TPU v7x, 32 devices: a whole 2x2x4 slice. The times are simulated.
32 devices in a mesh: fsdp: 32 (over z, y, x, core).
Axes of the slice: x: 2, y: 2, z: 4, core: 2. Of those that a mesh axis runs over, the one named last changes fastest.
Arguments:
- token_ids: int32 [65536], P('fsdp'), may hold values from 0 to 14591
- masked: int32 [65536], P('fsdp'), may hold values 0 or 1
- swap_kind: int32 [65536], P('fsdp'), may hold values from 0 to 9
- swap_ids: int32 [65536], P('fsdp'), may hold values from 0 to 14591
- out_grad: bfloat16 [65536, 768], P('fsdp'), may hold values from -6 to 6
- embed_table: float32 [15104, 768], P('fsdp'), may hold values from -6 to 6
- table_first: float32 [15104, 768], P('fsdp'), may hold values from -16 to 16
- table_second: float32 [15104, 768], P('fsdp'), may hold values from 10 to 10000
- layer_mats: float32 [768, 9216], P(None, 'fsdp'), may hold values from -4 to 4
- mats_first: float32 [768, 9216], P(None, 'fsdp'), may hold values from -16 to 16
- mats_second: float32 [768, 9216], P(None, 'fsdp'), may hold values from 10 to 10000
- layer_vecs: float32 [9216], P('fsdp'), may hold values from -1.2 to 1.9
- vecs_first: float32 [9216], P('fsdp'), may hold values from -16 to 16
- vecs_second: float32 [9216], P('fsdp'), may hold values from 10 to 10000
Outputs:
- layer_out: bfloat16 [65536, 768], P('fsdp')
- input_grad: bfloat16 [65536, 768], P('fsdp')
- table_grad: float32 [15104, 768], P('fsdp')
- mats_grad: float32 [768, 9216], P(None, 'fsdp')
- vecs_grad: float32 [9216], P('fsdp')
- table_step: float32 [15104, 768], P('fsdp')
- table_first_next: float32 [15104, 768], P('fsdp')
- mats_step: float32 [768, 9216], P(None, 'fsdp')
- mats_first_next: float32 [768, 9216], P(None, 'fsdp')
- vecs_step: float32 [9216], P('fsdp')
- vecs_first_next: float32 [9216], P('fsdp')
Inputs may be any that keep to these rules, and one draw needn't show every extreme that they name: `swap_kind`: kinds 0 to 7 mean the mask token 103, kind 8 the id of swap_ids, kind 9 keeps the token's own id.
All inputs are finite; a program needn't handle non-finite values. No bound on the sum of `masked` on one device may be relied on, other than what follows from the above.
Results may differ from a plain program's by a relative error of at most 0.015.
The roundings to bfloat16 on the way count: a program that leaves them out, or rounds other values in their place, can miss the bound.
Values may be sent and summed in bfloat16 or wider, within the bound.
A program may use at most 320 MiB of HBM per device.

v0:
```python
import functools

import jax
import jax.numpy as jnp
from jax import lax
from jax.experimental import pallas as pl
from jax.experimental.pallas import tpu as pltpu
from jax.sharding import PartitionSpec as P

D = 768
HEADS = 12
HEAD_DIM = 64
FF = 3072
VOCAB = 14592
LENGTH = 512
STEP = 10
QKV = 3 * D

norm_eps = 1e-12
mask_token = 103
beta_one = 0.9
beta_two = 0.999
adam_eps = 1e-06
decay_rate = 0.01

BF = jnp.bfloat16
F32 = jnp.float32
LOG2E = 1.4426950408889634
SCORE = HEAD_DIM ** (-0.5)
MB = 1024 * 1024

ROW_TILE = 256
FF_TILE = 768


def dot_nn(left, right):
    return lax.dot_general(
        left, right, (((1,), (0,)), ((), ())), preferred_element_type=F32
    )


def dot_nt(left, right):
    return lax.dot_general(
        left, right, (((1,), (1,)), ((), ())), preferred_element_type=F32
    )


def dot_tn(left, right):
    return lax.dot_general(
        left, right, (((0,), (0,)), ((), ())), preferred_element_type=F32
    )


def attention_forward_kernel(q_ref, k_ref, v_ref, att_ref, lse_ref):
    query = q_ref[...]
    keys = k_ref[...]
    values_t = v_ref[...].T
    lane = lax.broadcasted_iota(jnp.int32, query.shape, 1)
    outs = []
    for half in range(2):
        mine = (lane < HEAD_DIM) if half == 0 else (lane >= HEAD_DIM)
        picked = jnp.where(mine, query, jnp.zeros_like(query))
        scores = dot_nt(keys, picked)
        highest = jnp.max(scores, 0, keepdims=True)
        expo = jnp.exp2((scores - highest) * (SCORE * LOG2E))
        total = jnp.sum(expo, 0, keepdims=True)
        part = values_t[half * HEAD_DIM : (half + 1) * HEAD_DIM, :]
        outs.append(dot_nn(part, expo.astype(BF)) / total)
        lse_ref[0, half : half + 1, :] = highest * (SCORE * LOG2E) + jnp.log2(total)
    att_ref[...] = jnp.concatenate(outs, 0).T.astype(BF)


def attention_forward(projected):
    rows = projected.shape[0]
    seqs = rows // LENGTH
    pairs = HEADS // 2
    block = (LENGTH, 2 * HEAD_DIM)
    return pl.pallas_call(
        attention_forward_kernel,
        grid=(seqs, pairs),
        in_specs=[
            pl.BlockSpec(block, lambda s, h: (s, h)),
            pl.BlockSpec(block, lambda s, h: (s, pairs + h)),
            pl.BlockSpec(block, lambda s, h: (s, 2 * pairs + h)),
        ],
        out_specs=[
            pl.BlockSpec(block, lambda s, h: (s, h)),
            pl.BlockSpec((1, 2, LENGTH), lambda s, h: (s * pairs + h, 0, 0)),
        ],
        out_shape=[
            jax.ShapeDtypeStruct((rows, D), BF),
            jax.ShapeDtypeStruct((seqs * pairs, 2, LENGTH), F32),
        ],
        compiler_params=pltpu.CompilerParams(vmem_limit_bytes=48 * MB),
        name="attention_forward",
    )(projected, projected, projected)


def gelu_parts(values):
    size = jnp.abs(values)
    frac = 1.0 / (1.0 + (0.3275911 * 0.7071067811865476) * size)
    expo = jnp.exp2(values * values * (-0.5 * LOG2E))
    poly = 1.061405429 * 0.5
    for coef in (-1.453152027, 1.421413741, -0.284496736, 0.254829592):
        poly = poly * frac + 0.5 * coef
    tail = poly * frac * expo
    cdf = jnp.where(values >= 0, 1.0 - tail, tail)
    return values * cdf, cdf + values * expo * 0.3989422804014327


def norm_parts(total):
    centre = jnp.mean(total, -1, keepdims=True)
    centered = total - centre
    variance = jnp.mean(centered * centered, -1, keepdims=True)
    scale = lax.rsqrt(variance + norm_eps)
    return centered * scale, scale


def norm_back(scaled, unit, scale):
    return scale * (
        scaled
        - jnp.mean(scaled, -1, keepdims=True)
        - unit * jnp.mean(scaled * unit, -1, keepdims=True)
    )


def middle_kernel(
    att_ref,
    x_ref,
    go_ref,
    mask_ref,
    wout_ref,
    wup_ref,
    wdown_ref,
    vec_ref,
    bup_ref,
    out_ref,
    normed_ref,
    hidden_ref,
    gmid_ref,
    gup_ref,
    gfirst_ref,
    gfirstb_ref,
    gatt_ref,
    sums_ref,
    slope_ref,
):
    @pl.when(pl.program_id(0) == 0)
    def _():
        sums_ref[...] = jnp.zeros_like(sums_ref)

    bias_out = vec_ref[0:1, :]
    gain_one = vec_ref[1:2, :]
    shift_one = vec_ref[2:3, :]
    bias_down = vec_ref[3:4, :]
    gain_two = vec_ref[4:5, :]
    shift_two = vec_ref[5:6, :]

    def note(row, values):
        sums_ref[row : row + 1, 0:D] += jnp.sum(values, 0, keepdims=True)

    branch = dot_nt(att_ref[...], wout_ref[...]) + bias_out
    unit_one, scale_one = norm_parts(x_ref[...] + branch)
    normed = unit_one * gain_one + shift_one
    normed_b = normed.astype(BF)
    normed_ref[...] = normed_b
    downward = jnp.zeros(normed.shape, F32)
    for start in range(0, FF, FF_TILE):
        cols = slice(start, start + FF_TILE)
        upward = dot_nt(normed_b, wup_ref[cols, :]) + bup_ref[0:1, cols]
        hidden, slope = gelu_parts(upward)
        slope_ref[:, cols] = slope
        hidden_b = hidden.astype(BF)
        hidden_ref[:, cols] = hidden_b
        downward += dot_nn(hidden_b, wdown_ref[cols, :])
    unit_two, scale_two = norm_parts(normed + downward + bias_down)
    out_ref[...] = (unit_two * gain_two + shift_two).astype(BF)
    g_out = go_ref[...].astype(F32) * mask_ref[...].astype(F32)
    note(5, g_out * unit_two)
    note(6, g_out)
    g_mid = norm_back(g_out * gain_two, unit_two, scale_two)
    note(4, g_mid)
    g_mid_b = g_mid.astype(BF)
    gmid_ref[...] = g_mid_b
    g_normed = g_mid
    for start in range(0, FF, FF_TILE):
        cols = slice(start, start + FF_TILE)
        g_up = dot_nt(g_mid_b, wdown_ref[cols, :]) * slope_ref[:, cols]
        sums_ref[0:1, cols] += jnp.sum(g_up, 0, keepdims=True)
        g_up_b = g_up.astype(BF)
        gup_ref[:, cols] = g_up_b
        g_normed += dot_nn(g_up_b, wup_ref[cols, :])
    note(2, g_normed * unit_one)
    note(3, g_normed)
    g_first = norm_back(g_normed * gain_one, unit_one, scale_one)
    note(1, g_first)
    gfirst_ref[...] = g_first
    g_first_b = g_first.astype(BF)
    gfirstb_ref[...] = g_first_b
    gatt_ref[...] = dot_nn(g_first_b, wout_ref[...]).astype(BF)


def middle(attended, inputs, out_grad, masked, mats_t, vecs, bias_up):
    rows = attended.shape[0]
    tile = ROW_TILE

    def row(width):
        return pl.BlockSpec((tile, width), lambda i: (i, 0))

    def whole(shape, place=0):
        return pl.BlockSpec(
            shape, lambda i: (place, 0), pipeline_mode=pl.Buffered(buffer_count=1)
        )

    return pl.pallas_call(
        middle_kernel,
        grid=(rows // tile,),
        in_specs=[
            row(D),
            row(D),
            row(D),
            row(1),
            whole((D, D), 3),
            whole((FF, D), 1),
            whole((FF, D), 2),
            whole((8, D)),
            whole((1, FF)),
        ],
        out_specs=[
            row(D),
            row(D),
            row(FF),
            row(D),
            row(FF),
            row(D),
            row(D),
            row(D),
            pl.BlockSpec((8, FF), lambda i: (0, 0)),
        ],
        out_shape=[
            jax.ShapeDtypeStruct((rows, D), BF),
            jax.ShapeDtypeStruct((rows, D), BF),
            jax.ShapeDtypeStruct((rows, FF), BF),
            jax.ShapeDtypeStruct((rows, D), BF),
            jax.ShapeDtypeStruct((rows, FF), BF),
            jax.ShapeDtypeStruct((rows, D), F32),
            jax.ShapeDtypeStruct((rows, D), BF),
            jax.ShapeDtypeStruct((rows, D), BF),
            jax.ShapeDtypeStruct((8, FF), F32),
        ],
        scratch_shapes=[pltpu.VMEM((tile, FF), F32)],
        compiler_params=pltpu.CompilerParams(vmem_limit_bytes=56 * MB),
        name="middle",
    )(attended, inputs, out_grad, masked, mats_t, mats_t, mats_t, vecs, bias_up)


def entry_kernel(
    key_ref, found_ref, extra_ref, place_ref, w_ref, bias_ref, x_ref, xb_ref, proj_ref
):
    slots = lax.broadcasted_iota(jnp.int32, (LENGTH, found_ref.shape[0]), 1)
    picked = (key_ref[...] == slots).astype(BF)
    inputs = dot_nn(picked, found_ref[...]) + extra_ref[...].astype(F32)
    inputs = inputs + place_ref[...].astype(F32)
    x_ref[...] = inputs
    inputs_b = inputs.astype(BF)
    xb_ref[...] = inputs_b
    for start in range(0, QKV, D):
        cols = slice(start, start + D)
        part = dot_nt(inputs_b, w_ref[cols, :]) + bias_ref[:, cols]
        proj_ref[:, cols] = part.astype(BF)


def fixed(shape, place=0):
    return pl.BlockSpec(
        shape, lambda i: (place, 0), pipeline_mode=pl.Buffered(buffer_count=1)
    )


def entry(key, found, extra, places, mats_t, bias):
    rows = key.shape[0]
    slots = found.shape[0]

    def row(width):
        return pl.BlockSpec((LENGTH, width), lambda i: (i, 0))

    return pl.pallas_call(
        entry_kernel,
        grid=(rows // LENGTH,),
        in_specs=[
            row(1),
            fixed((slots, D)),
            row(D),
            fixed((LENGTH, D)),
            fixed((QKV, D)),
            fixed((1, QKV)),
        ],
        out_specs=[row(D), row(D), row(QKV)],
        out_shape=[
            jax.ShapeDtypeStruct((rows, D), F32),
            jax.ShapeDtypeStruct((rows, D), BF),
            jax.ShapeDtypeStruct((rows, QKV), BF),
        ],
        compiler_params=pltpu.CompilerParams(vmem_limit_bytes=56 * MB),
        cost_estimate=pl.CostEstimate(
            flops=13_000_000_000, bytes_accessed=40_000_000, transcendentals=0
        ),
        name="entry",
    )(key[:, None], found, extra, places, mats_t, bias)


def rest_kernel(first_ref, att_ref, up_ref, normed_ref, hidden_ref, mid_ref, out_ref):
    step = pl.program_id(0)
    chunks = FF // D

    @pl.when(step == 0)
    def _():
        out_ref[...] = dot_tn(first_ref[...], att_ref[...]).astype(BF)

    @pl.when(jnp.logical_and(step > 0, step <= chunks))
    def _():
        out_ref[...] = dot_tn(up_ref[...], normed_ref[...]).astype(BF)

    @pl.when(step > chunks)
    def _():
        out_ref[...] = dot_tn(hidden_ref[...], mid_ref[...]).astype(BF)


def rest_gradients(g_first_b, attended, g_up_b, normed_b, hidden_b, g_mid_b):
    rows = attended.shape[0]
    chunks = FF // D
    full = fixed((rows, D))
    return pl.pallas_call(
        rest_kernel,
        grid=(1 + 2 * chunks,),
        in_specs=[
            full,
            full,
            pl.BlockSpec((rows, D), lambda i: (0, jnp.clip(i - 1, 0, chunks - 1))),
            full,
            pl.BlockSpec((rows, D), lambda i: (0, jnp.clip(i - 1 - chunks, 0, chunks - 1))),
            full,
        ],
        out_specs=pl.BlockSpec((D, D), lambda i: (i, 0)),
        out_shape=jax.ShapeDtypeStruct((D + 2 * FF, D), BF),
        compiler_params=pltpu.CompilerParams(vmem_limit_bytes=56 * MB),
        cost_estimate=pl.CostEstimate(
            flops=22_000_000_000, bytes_accessed=50_000_000, transcendentals=0
        ),
        name="rest_gradients",
    )(g_first_b, attended, g_up_b, normed_b, hidden_b, g_mid_b)


MESH = pl.DeviceIdType.MESH
PLANES = 4


def neighbours():
    me = lax.axis_index("fsdp")
    core = lax.rem(me, 2)
    x = lax.rem(me // 2, 2)
    y = lax.rem(me // 4, 2)
    z = me // 8
    step_a = 4 - 2 * core
    step_b = 2 + 2 * core
    a = jnp.where(core == 0, y, x)
    b = jnp.where(core == 0, x, y)
    near_a = me + step_a * (1 - 2 * a)
    near_b = me + step_b * (1 - 2 * b)
    twin = me + 1 - 2 * core
    return me, core, z, a, b, step_a, step_b, near_a, near_b, twin


def greet(me, z, near_a, near_b, twin):
    barrier = pltpu.get_barrier_semaphore()

    def hello(device):
        pl.semaphore_signal(barrier, inc=1, device_id=(device,), device_id_type=MESH)

    for device in (near_a, near_b, twin):
        hello(device)

    @pl.when(z > 0)
    def _():
        hello(me - 8)

    @pl.when(z < PLANES - 1)
    def _():
        hello(me + 8)

    inner = jnp.logical_and(z > 0, z < PLANES - 1)
    pl.semaphore_wait(barrier, jnp.where(inner, 5, 4))


class RestSums:
    TURNS = PLANES - 1

    def __init__(self, in_ref, out_ref, scratch):
        self.in_ref, self.out_ref = in_ref, out_ref
        (
            self.own,
            self.from_twin,
            self.from_b,
            self.from_a,
            self.from_low,
            self.from_high,
            self.load_sem,
            self.twin_sem,
            self.b_sem,
            self.a_sem,
            self.low_sem,
            self.high_sem,
        ) = scratch
        self.place = neighbours()

    @staticmethod
    def scratch(shape):
        return [
            pltpu.VMEM((12,) + shape, BF),
            pltpu.VMEM((12,) + shape, BF),
            pltpu.VMEM((6,) + shape, BF),
            pltpu.VMEM((3,) + shape, BF),
            pltpu.VMEM((4,) + shape, BF),
            pltpu.VMEM((4,) + shape, BF),
            pltpu.SemaphoreType.DMA((12,)),
            pltpu.SemaphoreType.DMA((2, 12)),
            pltpu.SemaphoreType.DMA((2, 6)),
            pltpu.SemaphoreType.DMA((2, 3)),
            pltpu.SemaphoreType.DMA((2, 4)),
            pltpu.SemaphoreType.DMA((2, 4)),
        ]

    def remote(self, source, target, sems, slot, device):
        return pltpu.make_async_remote_copy(
            src_ref=source,
            dst_ref=target.at[slot],
            send_sem=sems.at[0, slot],
            recv_sem=sems.at[1, slot],
            device_id=(device,),
            device_id_type=MESH,
        )

    def plane_of(self, turn):
        z = self.place[2]
        last = PLANES - 1 - turn
        inner = (1, 3, 2)[turn]
        return jnp.where(z < 2, last, jnp.where(z == 2, inner, 1 + turn))

    def shards(self, slot):
        me, core, z, a, b, step_a, step_b, near_a, near_b, twin = self.place
        other_b, turn, other_a = slot < 6, slot % 6 // 2, slot % 2 == 0
        base = (self.plane_of(turn) - 1) * 8
        a_at = 1 - a if other_a else a
        b_at = 1 - b if other_b else b
        mine = base + a_at * step_a + b_at * step_b + core
        a_at = 1 - b if other_a else b
        b_at = 1 - a if other_b else a
        twins = base + a_at * step_b + b_at * step_a + 1 - core
        return mine, twins

    def load(self, slot):
        return pltpu.make_async_copy(
            self.in_ref.at[self.shards(slot)[0]], self.own.at[slot], self.load_sem.at[slot]
        )

    def gift(self, slot):
        return self.remote(
            self.in_ref.at[self.shards(slot)[1]],
            self.from_twin,
            self.twin_sem,
            slot,
            self.place[9],
        )

    def over_b(self, slot):
        return self.remote(self.own.at[slot], self.from_b, self.b_sem, slot, self.place[8])

    def over_a(self, turn):
        return self.remote(
            self.own.at[6 + 2 * turn], self.from_a, self.a_sem, turn, self.place[7]
        )

    def along(self, turn, up):
        plane = self.plane_of(turn)
        source = self.own.at[7 + 2 * turn]
        if up:
            return self.remote(source, self.from_low, self.low_sem, plane, self.place[0] + 8)
        return self.remote(source, self.from_high, self.high_sem, plane, self.place[0] - 8)

    def add(self, slot, arrived):
        self.own[slot] = (self.own[slot].astype(F32) + arrived[...].astype(F32)).astype(BF)

    def start(self):
        me, core, z, a, b, step_a, step_b, near_a, near_b, twin = self.place
        greet(me, z, near_a, near_b, twin)
        for slot in (0, 1, 2, 3, 6, 7, 4, 5, 8, 9, 10, 11):
            self.gift(slot).start()
            self.load(slot).start()

    def far(self, turn):
        for slot in (2 * turn, 2 * turn + 1):
            self.load(slot).wait()
            self.gift(slot).wait_recv()
            self.add(slot, self.from_twin.at[slot])
            self.over_b(slot).start()

    def near(self, turn):
        for slot in (6 + 2 * turn, 7 + 2 * turn):
            self.load(slot).wait()
            self.gift(slot).wait_recv()
            self.add(slot, self.from_twin.at[slot])

    def stage_b(self, turn):
        for slot in (2 * turn, 2 * turn + 1):
            self.over_b(slot).wait_recv()
            self.add(6 + slot, self.from_b.at[slot])
        self.over_a(turn).start()

    def stage_a(self, turn):
        z = self.place[2]
        slot = 7 + 2 * turn
        plane = self.plane_of(turn)
        self.over_a(turn).wait_recv()
        self.add(slot, self.from_a.at[turn])

        @pl.when(jnp.logical_and(plane > z, z > 0))
        def _():
            self.along(turn, True).wait_recv()
            self.add(slot, self.from_low.at[plane])

        @pl.when(plane > z)
        def _():
            self.along(turn, True).start()

        @pl.when(jnp.logical_and(plane < z, z < PLANES - 1))
        def _():
            self.along(turn, False).wait_recv()
            self.add(slot, self.from_high.at[plane])

        @pl.when(plane < z)
        def _():
            self.along(turn, False).start()

        @pl.when(plane == z)
        def _():
            self.along(turn, True).wait_recv()
            self.out_ref[...] = self.own[slot].astype(F32) + self.from_low[plane].astype(F32)

        @pl.when(jnp.logical_and(plane == z, z < PLANES - 1))
        def _():
            self.along(turn, False).wait_recv()
            self.out_ref[...] += self.from_high[plane].astype(F32)

    def end(self):
        z = self.place[2]
        for slot in range(12):
            self.gift(slot).wait_send()
        for slot in range(6):
            self.over_b(slot).wait_send()
        for turn in range(self.TURNS):
            self.over_a(turn).wait_send()
            plane = self.plane_of(turn)

            @pl.when(plane > z)
            def _(turn=turn):
                self.along(turn, True).wait_send()

            @pl.when(plane < z)
            def _(turn=turn):
                self.along(turn, False).wait_send()

    def schedule(self):
        return {
            0: [self.start],
            1: [lambda: self.far(0)],
            2: [lambda: self.far(1)],
            3: [lambda: self.near(0)],
            4: [lambda: self.far(2)],
            5: [lambda: self.near(1)],
            6: [lambda: self.near(2)],
            7: [lambda: self.stage_b(0)],
            11: [lambda: self.stage_b(1)],
            13: [lambda: self.stage_a(0)],
            16: [lambda: self.stage_b(2)],
            19: [lambda: self.stage_a(1)],
            24: [lambda: self.stage_a(2)],
            27: [self.end],
        }


PIECES = 4


def share_places_kernel(split, table_ref, out_ref, stage, load_sem, send_sem, recv_sem):
    first_owner, first_row, count = split
    me, core, z, a, b, step_a, step_b, near_a, near_b, twin = neighbours()
    greet(me, z, near_a, near_b, twin)
    rows = LENGTH // PIECES
    root = first_owner + 1
    gift = pltpu.make_async_remote_copy(
        src_ref=table_ref.at[pl.ds(first_row, count)],
        dst_ref=stage.at[pl.ds(0, count)],
        send_sem=load_sem.at[0],
        recv_sem=load_sem.at[1],
        device_id=(root,),
        device_id_type=MESH,
    )
    mine = pltpu.make_async_copy(
        table_ref.at[pl.ds(0, LENGTH - count)],
        stage.at[pl.ds(count, LENGTH - count)],
        load_sem.at[2],
    )

    @pl.when(me == first_owner)
    def _():
        gift.start()

    @pl.when(me == root)
    def _():
        mine.start()
        mine.wait()
        gift.wait_recv()

    def copy(piece, device, kind):
        part = pl.ds(piece * rows, rows)
        return pltpu.make_async_remote_copy(
            src_ref=out_ref.at[part],
            dst_ref=out_ref.at[part],
            send_sem=send_sem.at[kind, piece],
            recv_sem=recv_sem.at[piece],
            device_id=(device,),
            device_id_type=MESH,
        )

    trunk = jnp.logical_and(core == 1, jnp.logical_and(a == 1, b == 1))
    branch = jnp.logical_and(core == 1, jnp.logical_and(a == 0, b == 1))
    routes = (
        (jnp.logical_and(trunk, z > 0), me - 8),
        (trunk, near_a),
        (jnp.logical_or(trunk, branch), near_b),
        (core == 1, twin),
    )
    for piece in range(PIECES):
        part = slice(piece * rows, (piece + 1) * rows)

        @pl.when(me == root)
        def _(part=part):
            out_ref[part, :] = stage[part, :].astype(BF)

        @pl.when(me != root)
        def _(piece=piece):
            copy(piece, twin, 3).wait_recv()

        for kind, (goes, device) in enumerate(routes):

            @pl.when(goes)
            def _(piece=piece, device=device, kind=kind):
                copy(piece, device, kind).start()

    for piece in range(PIECES):
        for kind, (goes, device) in enumerate(routes):

            @pl.when(goes)
            def _(piece=piece, device=device, kind=kind):
                copy(piece, device, kind).wait_send()

    @pl.when(me == first_owner)
    def _():
        gift.wait_send()


def place_split(devices, owned):
    first_owner = VOCAB // owned
    first_row = VOCAB - first_owner * owned
    return first_owner, first_row, owned - first_row


def share_places(table, split, ident):
    return pl.pallas_call(
        functools.partial(share_places_kernel, split),
        in_specs=[pl.BlockSpec(memory_space=pl.ANY)],
        out_specs=pl.BlockSpec(memory_space=pltpu.VMEM),
        out_shape=jax.ShapeDtypeStruct((LENGTH, D), BF),
        scratch_shapes=[
            pltpu.VMEM((LENGTH, D), F32),
            pltpu.SemaphoreType.DMA((3,)),
            pltpu.SemaphoreType.DMA((4, PIECES)),
            pltpu.SemaphoreType.DMA((PIECES,)),
        ],
        compiler_params=pltpu.CompilerParams(collective_id=ident, has_side_effects=True),
        cost_estimate=pl.CostEstimate(flops=0, bytes_accessed=60_000_000, transcendentals=0),
        name="share_places",
    )(table)


CHUNKS = 3


def homecoming_kernel(
    split,
    place_ref,
    first_ref,
    out_ref,
    mats_ref,
    sums,
    from_twin,
    from_b,
    from_a,
    from_z,
    ready,
    own,
    own_twin,
    own_b,
    own_a,
    own_high,
    sems,
    z_sem,
    piece_sem,
    home_sem,
    load_sem,
    twin_sem,
    b_sem,
    a_sem,
    high_sem,
):
    first_owner, first_row, count = split
    root = first_owner + 1
    me, core, z, a, b, step_a, step_b, near_a, near_b, twin = neighbours()
    rows = place_ref.shape[4]
    height = first_ref.shape[1] // CHUNKS
    out_ref[...] = jnp.zeros_like(out_ref)
    barrier = pltpu.get_barrier_semaphore()

    def each(step, carry):
        pl.semaphore_signal(
            barrier, inc=1, device_id=(lax.rem(me + step, 32),), device_id_type=MESH
        )
        return carry

    lax.fori_loop(1, 32, each, 0)
    pl.semaphore_wait(barrier, 31)

    def remote(source, target, send, receive, device):
        return pltpu.make_async_remote_copy(
            src_ref=source,
            dst_ref=target,
            send_sem=send,
            recv_sem=receive,
            device_id=(device,),
            device_id_type=MESH,
        )

    def add(total, extra):
        return (total.astype(F32) + extra.astype(F32)).astype(BF)

    x = jnp.where(core == 0, b, a)
    y = jnp.where(core == 0, a, b)
    gift = remote(place_ref.at[:, :, :, 1 - core], from_twin, sems.at[0, 0], sems.at[0, 1], twin)
    gift.start()
    loads, gifts = [], []
    for slot in range(4):
        other_b, other_a = slot < 2, slot % 2 == 0
        a_at, b_at = (1 - a if other_a else a), (1 - b if other_b else b)
        shard = a_at * step_a + b_at * step_b + core
        loads.append(pltpu.make_async_copy(first_ref.at[shard], own.at[slot], load_sem.at[slot]))
        a_at, b_at = (1 - b if other_a else b), (1 - a if other_b else a)
        shard = a_at * step_b + b_at * step_a + 1 - core
        gifts.append(
            remote(
                first_ref.at[shard],
                own_twin.at[slot],
                twin_sem.at[0, slot],
                twin_sem.at[1, slot],
                twin,
            )
        )
    for slot in range(4):
        gifts[slot].start()
        loads[slot].start()
    gift.wait_recv()
    sums[...] = add(place_ref[:, :, :, core], from_twin[...])

    @pl.when(core == 0)
    def _():
        remote(sums.at[:, :, 1 - x], from_b, sems.at[1, 0], sems.at[1, 1], near_b).start()

    @pl.when(core == 1)
    def _():
        remote(sums.at[:, 1 - y], from_b, sems.at[1, 0], sems.at[1, 1], near_b).start()

    over_b = [
        remote(own.at[slot], own_b.at[slot], b_sem.at[0, slot], b_sem.at[1, slot], near_b)
        for slot in range(2)
    ]
    for slot in range(4):
        loads[slot].wait()
        gifts[slot].wait_recv()
        own[slot] = add(own[slot], own_twin[slot])
        if slot < 2:
            over_b[slot].start()

    small_b = remote(sums.at[:, 0], from_b, sems.at[1, 0], sems.at[1, 1], near_b)
    small_b.wait_recv()

    @pl.when(core == 0)
    def _():
        from_b[...] = add(sums[:, :, x], from_b[...])

    @pl.when(core == 1)
    def _():
        from_b[...] = add(sums[:, y], from_b[...])

    small_a = remote(from_b.at[:, 1 - a], from_a, sems.at[2, 0], sems.at[2, 1], near_a)
    small_a.start()
    over_a = remote(own.at[2], own_a, a_sem.at[0], a_sem.at[1], near_a)
    for slot in range(2):
        over_b[slot].wait_recv()
        own[2 + slot] = add(own[2 + slot], own_b[slot])
        if slot == 0:
            over_a.start()
    small_a.wait_recv()
    from_a[...] = add(from_b[:, a], from_a[...])

    def column(plane, action):
        @pl.when(plane != z)
        def _():
            action(
                remote(
                    from_a.at[plane],
                    from_z.at[z],
                    z_sem.at[0, plane],
                    z_sem.at[1, z],
                    me + 8 * (plane - z),
                )
            )

    for plane in range(PLANES):
        column(plane, lambda item: item.start())
    over_a.wait_recv()

    def down(chunk):
        part = pl.ds(chunk * height, height)
        return remote(
            own.at[3, part],
            own_high.at[part],
            high_sem.at[0, chunk],
            high_sem.at[1, chunk],
            me - 8,
        )

    for chunk in range(CHUNKS):
        part = pl.ds(chunk * height, height)
        own[3, part] = add(own[3, part], own_a[part])

        @pl.when(z < PLANES - 1)
        def _(chunk=chunk, part=part):
            down(chunk).wait_recv()
            own[3, part] = add(own[3, part], own_high[part])

        @pl.when(z > 0)
        def _(chunk=chunk):
            down(chunk).start()

    mats_ref[...] = own[3].astype(F32)
    ready[...] = from_a[z].astype(F32)
    for plane in range(PLANES):

        @pl.when(plane != z)
        def _(plane=plane):
            remote(
                from_a.at[plane], from_z.at[plane], z_sem.at[0, plane], z_sem.at[1, plane], twin
            ).wait_recv()
            ready[...] += from_z[plane].astype(F32)

    def home(device, half):
        place = device * rows + half * 8
        early = place < count
        owner = jnp.where(early, first_owner, root)
        spot = pl.multiple_of(jnp.where(early, first_row + place, place - count), 8)
        return owner, spot

    def piece(device, half):
        owner, spot = home(device, half)
        return remote(
            ready.at[pl.ds(half * 8, 8)],
            out_ref.at[pl.ds(spot, 8)],
            piece_sem.at[half],
            home_sem.at[device * 2 + half],
            owner,
        )

    for half in range(2):
        owner, spot = home(me, half)

        @pl.when(owner == me)
        def _(half=half, spot=spot):
            out_ref[pl.ds(spot, 8), :] = ready[half * 8 : half * 8 + 8, :]

        @pl.when(owner != me)
        def _(half=half):
            piece(me, half).start()

    def arrive(index, carry):
        device, half = index // 2, lax.rem(index, 2)
        owner, _ = home(device, half)

        @pl.when(jnp.logical_and(owner == me, device != me))
        def _():
            piece(device, half).wait_recv()

        return carry

    @pl.when(me >= first_owner)
    def _():
        lax.fori_loop(0, 64, arrive, 0)

    for half in range(2):
        owner, _ = home(me, half)

        @pl.when(owner != me)
        def _(half=half):
            piece(me, half).wait_send()

    for item in [gift, small_b, small_a, over_a] + gifts + over_b:
        item.wait_send()
    for plane in range(PLANES):
        column(plane, lambda item: item.wait_send())
    for chunk in range(CHUNKS):

        @pl.when(z > 0)
        def _(chunk=chunk):
            down(chunk).wait_send()


def homecoming(place_sums, first, owned, split, ident):
    rows = LENGTH // 32
    small = (rows, D)
    shape = first.shape[1:]
    return pl.pallas_call(
        functools.partial(homecoming_kernel, split),
        in_specs=[
            pl.BlockSpec(memory_space=pltpu.VMEM),
            pl.BlockSpec(memory_space=pl.ANY),
        ],
        out_specs=[pl.BlockSpec(memory_space=pltpu.VMEM)] * 2,
        out_shape=[
            jax.ShapeDtypeStruct((owned, D), F32),
            jax.ShapeDtypeStruct(shape, F32),
        ],
        scratch_shapes=[
            pltpu.VMEM((4, 2, 2) + small, BF),
            pltpu.VMEM((4, 2, 2) + small, BF),
            pltpu.VMEM((4, 2) + small, BF),
            pltpu.VMEM((4,) + small, BF),
            pltpu.VMEM((4,) + small, BF),
            pltpu.VMEM(small, F32),
            pltpu.VMEM((4,) + shape, BF),
            pltpu.VMEM((4,) + shape, BF),
            pltpu.VMEM((2,) + shape, BF),
            pltpu.VMEM(shape, BF),
            pltpu.VMEM(shape, BF),
            pltpu.SemaphoreType.DMA((3, 2)),
            pltpu.SemaphoreType.DMA((2, 4)),
            pltpu.SemaphoreType.DMA((2,)),
            pltpu.SemaphoreType.DMA((64,)),
            pltpu.SemaphoreType.DMA((4,)),
            pltpu.SemaphoreType.DMA((2, 4)),
            pltpu.SemaphoreType.DMA((2, 2)),
            pltpu.SemaphoreType.DMA((2,)),
            pltpu.SemaphoreType.DMA((2, CHUNKS)),
        ],
        compiler_params=pltpu.CompilerParams(
            collective_id=ident, has_side_effects=True, vmem_limit_bytes=40 * MB
        ),
        cost_estimate=pl.CostEstimate(
            flops=0, bytes_accessed=200_000_000, transcendentals=0
        ),
        name="homecoming",
    )(place_sums.reshape((4, 2, 2, 2) + small), first)


def backward_kernel(
    by_kernel,
    q_ref,
    k_ref,
    v_ref,
    att_ref,
    g_ref,
    lse_ref,
    first_ref,
    xb_ref,
    w_ref,
    rest_ref,
    grad_ref,
    place_ref,
    weights_ref,
    bias_ref,
    mats_ref,
    proj,
    total,
    places,
    *scratch,
):
    seq, head = pl.program_id(0), pl.program_id(1)
    pairs = HEADS // 2
    step = seq * (pairs + 1) + head

    @pl.when(step == 0)
    def _():
        total[...] = jnp.zeros_like(total)
        places[...] = jnp.zeros_like(places)
        bias_ref[...] = jnp.zeros_like(bias_ref)
        mats_ref[...] = jnp.zeros_like(mats_ref)

    if by_kernel:
        sums = RestSums(rest_ref, mats_ref, scratch)
        for when, actions in sums.schedule().items():

            @pl.when(step == when)
            def _(actions=actions):
                for action in actions:
                    action()

    @pl.when(head < pairs)
    def _():
        cols = pl.ds(pl.multiple_of(head * 2 * HEAD_DIM, 2 * HEAD_DIM), 2 * HEAD_DIM)
        query = q_ref[...]
        keys = k_ref[...]
        values = v_ref[...]
        grad = g_ref[...]
        lane = lax.broadcasted_iota(jnp.int32, query.shape, 1)
        first = lane < HEAD_DIM
        product = (att_ref[...].astype(F32) * grad.astype(F32)).T
        zero = jnp.zeros_like(query)
        g_q, g_k, g_v = [], [], []
        for half in range(2):
            mine = first if half == 0 else jnp.logical_not(first)
            scores = dot_nt(keys, jnp.where(mine, query, zero))
            probs = jnp.exp2(scores * (SCORE * LOG2E) - lse_ref[0, half : half + 1, :])
            delta = jnp.sum(
                product[half * HEAD_DIM : (half + 1) * HEAD_DIM, :], 0, keepdims=True
            )
            g_probs = dot_nt(values, jnp.where(mine, grad, zero))
            g_v.append(dot_nn(probs.astype(BF), grad))
            g_scores = (probs * (g_probs - delta)).astype(BF)
            g_k.append(dot_nn(g_scores, query))
            g_q.append(dot_tn(g_scores, keys))
        grad_q = jnp.where(first, g_q[0], g_q[1]) * SCORE
        grad_k = jnp.where(first, g_k[0], g_k[1]) * SCORE
        grad_v = jnp.where(first, g_v[0], g_v[1])
        proj[0, :, cols] = grad_q.astype(BF)
        proj[1, :, cols] = grad_k.astype(BF)
        proj[2, :, cols] = grad_v.astype(BF)
        bias_ref[0:1, cols] += jnp.sum(grad_q, 0, keepdims=True)
        bias_ref[1:2, cols] += jnp.sum(grad_v, 0, keepdims=True)

    @pl.when(head == pairs)
    def _():
        g_in = first_ref[...]
        inputs_b = xb_ref[...]
        for part in range(3):
            cols = slice(part * D, (part + 1) * D)
            g_in = g_in + dot_nn(proj[part], w_ref[cols, :])
            total[cols, :] += dot_tn(proj[part], inputs_b)
        grad_ref[...] = g_in.astype(BF)
        places[...] += g_in

    @pl.when(step == pl.num_programs(0) * (pairs + 1) - 1)
    def _():
        weights_ref[...] = total[...].astype(BF)
        place_ref[...] = places[...].astype(BF)


def backward(by_kernel, projected, attended, grad_att, lse, g_first, inputs_b, mats_t, rest, ident):
    rows = projected.shape[0]
    seqs = rows // LENGTH
    pairs = HEADS // 2
    block = (LENGTH, 2 * HEAD_DIM)
    shape = rest.shape[1:]

    def pair(offset):
        return pl.BlockSpec(block, lambda s, h: (s, offset + jnp.minimum(h, pairs - 1)))

    def row(width):
        return pl.BlockSpec((LENGTH, width), lambda s, h: (s, 0))

    def steady(shape):
        return pl.BlockSpec(
            shape, lambda s, h: (0, 0), pipeline_mode=pl.Buffered(buffer_count=1)
        )

    def kept(shape):
        return pl.BlockSpec(shape, lambda s, h: (0, 0))

    return pl.pallas_call(
        functools.partial(backward_kernel, by_kernel),
        grid=(seqs, pairs + 1),
        in_specs=[
            pair(0),
            pair(pairs),
            pair(2 * pairs),
            pair(0),
            pair(0),
            pl.BlockSpec(
                (1, 2, LENGTH), lambda s, h: (s * pairs + jnp.minimum(h, pairs - 1), 0, 0)
            ),
            row(D),
            row(D),
            steady((QKV, D)),
            pl.BlockSpec(memory_space=pl.ANY),
        ],
        out_specs=[
            row(D),
            kept((LENGTH, D)),
            kept((QKV, D)),
            kept((8, D)),
            kept(shape),
        ],
        out_shape=[
            jax.ShapeDtypeStruct((rows, D), BF),
            jax.ShapeDtypeStruct((LENGTH, D), BF),
            jax.ShapeDtypeStruct((QKV, D), BF),
            jax.ShapeDtypeStruct((8, D), F32),
            jax.ShapeDtypeStruct(shape, F32),
        ],
        scratch_shapes=[
            pltpu.VMEM((3, LENGTH, D), BF),
            pltpu.VMEM((QKV, D), F32),
            pltpu.VMEM((LENGTH, D), F32),
        ]
        + (RestSums.scratch(shape) if by_kernel else []),
        compiler_params=pltpu.CompilerParams(
            vmem_limit_bytes=60 * MB,
            **(dict(collective_id=ident, has_side_effects=True) if by_kernel else {}),
        ),
        cost_estimate=pl.CostEstimate(
            flops=60_000_000_000, bytes_accessed=60_000_000, transcendentals=0
        ),
        name="backward",
    )(
        projected,
        projected,
        projected,
        attended,
        grad_att,
        lse,
        g_first,
        inputs_b,
        mats_t,
        rest,
    )


def slots_of(ids, owned):
    count = ids.shape[0]
    order = jnp.arange(count, dtype=jnp.int32)
    repeated = jnp.any(
        (ids[:, None] == ids[None, :]) & (order[:, None] < order[None, :]), axis=0
    )
    first = jnp.logical_not(repeated)
    base = (ids // owned) * owned
    below = (
        first[:, None]
        & (ids[:, None] >= base[None, :])
        & (ids[:, None] < ids[None, :])
    )
    return jnp.sum(below.astype(jnp.int32), axis=0)


def requests_of(ids, owner, slot, owned, devices, start, room):
    key = jnp.where((slot >= start) & (slot < start + room), owner * room + slot - start, -1)
    spots = jnp.arange(devices * room, dtype=jnp.int32)
    asked = jnp.max(
        jnp.where(key[:, None] == spots[None, :], (ids - owner * owned)[:, None], -1), axis=0
    )
    return key, asked


def pick(index, amount):
    return (index[:, None] == jnp.arange(amount, dtype=jnp.int32)[None, :]).astype(BF)


def adam_direction(param, first, second, grad, corr_one, corr_two, decay):
    first_next = beta_one * first + (1.0 - beta_one) * grad
    second_next = beta_two * second + (1.0 - beta_two) * grad * grad
    update = first_next / corr_one / (jnp.sqrt(second_next / corr_two) + adam_eps)
    return (update + decay * param, first_next)


def body(
    devices,
    token_ids,
    masked,
    swap_kind,
    swap_ids,
    out_grad,
    embed_table,
    table_first,
    table_second,
    layer_mats,
    mats_first,
    mats_second,
    layer_vecs,
    vecs_first,
    vecs_second,
):
    axis = "fsdp"
    rows = token_ids.shape[0]
    owned = embed_table.shape[0]
    entries = layer_vecs.shape[0]
    columns = layer_mats.shape[1]
    me = lax.axis_index(axis)
    by_kernel = devices == 32
    split = place_split(devices, owned)
    replaced = jnp.where(swap_kind < 8, mask_token, jnp.where(swap_kind == 8, swap_ids, token_ids))
    chosen = jnp.where(masked == 1, replaced, token_ids)

    def swap(blocks):
        return lax.all_to_all(blocks, axis, 0, 0, tiled=True)

    mats_t = lax.all_gather(layer_mats.astype(BF).T, axis, axis=0, tiled=True)

    room = 16 * -(-1536 // (16 * devices))
    more = 16
    owner = chosen // owned
    slot = slots_of(chosen, owned)
    most = jnp.max(slot) + 1
    key, asked = requests_of(chosen, owner, slot, owned, devices, 0, room)
    table_b = embed_table.astype(BF)
    own_vecs = layer_vecs.astype(BF).astype(F32)
    notes = jnp.concatenate(
        [
            asked.reshape(devices, room).astype(F32),
            jnp.broadcast_to(own_vecs[None], (devices, entries)),
            jnp.broadcast_to(most.astype(F32), (devices, 1)),
        ],
        axis=1,
    )
    notes = swap(notes)
    wanted = notes[:, :room].astype(jnp.int32).reshape(-1)
    vecs = notes[:, room : room + entries].reshape(-1)
    longest = jnp.max(notes[:, room + entries]).astype(jnp.int32)
    found = dot_nn(pick(wanted, owned), table_b).astype(BF)
    found = swap(found.reshape(devices, room, D)).reshape(-1, D)
    if by_kernel:
        places = share_places(embed_table, split, 1)
    else:
        spots = VOCAB + jnp.arange(LENGTH, dtype=jnp.int32) - me * owned
        places = lax.psum(dot_nn(pick(spots, owned), table_b), axis).astype(BF)
    rounds = (longest - room + more - 1) // more

    def fetch_more(state):
        turn, extra = state
        key, asked = requests_of(chosen, owner, slot, owned, devices, room + turn * more, more)
        wanted = swap(asked.reshape(devices, more)).reshape(-1)
        found = dot_nn(pick(wanted, owned), table_b).astype(BF)
        found = swap(found.reshape(devices, more, D)).reshape(-1, D)
        return turn + 1, extra + dot_nn(pick(key, devices * more), found).astype(BF)

    _, extra = lax.while_loop(
        lambda state: state[0] < rounds, fetch_more, (jnp.int32(0), jnp.zeros((rows, D), BF))
    )

    bias_qkv = jnp.concatenate([vecs[:D], jnp.zeros((D,), F32), vecs[D : 2 * D]])[None]
    bias_up = vecs[5 * D : 5 * D + FF][None]
    small = jnp.concatenate(
        [vecs[2 * D : 5 * D], vecs[5 * D + FF :], jnp.zeros((2 * D,), F32)]
    ).reshape(8, D)

    inputs, inputs_b, projected = entry(key, found, extra, places, mats_t, bias_qkv)
    attended, lse = attention_forward(projected)
    (
        outputs,
        normed_b,
        hidden_b,
        g_mid_b,
        g_up_b,
        g_first,
        g_first_b,
        g_att_b,
        sums,
    ) = middle(attended, inputs, out_grad, masked[:, None], mats_t, small, bias_up)
    g_rest = rest_gradients(g_first_b, attended, g_up_b, normed_b, hidden_b, g_mid_b)
    input_grad, g_places, g_qkv, bias_sums, rest_grad = backward(
        by_kernel,
        projected,
        attended,
        g_att_b,
        lse,
        g_first,
        inputs_b,
        mats_t,
        g_rest.reshape(-1, columns, D),
        2,
    )

    sent = dot_tn(pick(key, devices * room), input_grad).astype(BF)
    g_vecs = jnp.concatenate(
        [
            bias_sums[0],
            bias_sums[1],
            sums[1, :D],
            sums[2, :D],
            sums[3, :D],
            sums[0],
            sums[4, :D],
            sums[5, :D],
            sums[6, :D],
        ]
    )
    vecs_grad = jnp.sum(swap(g_vecs.reshape(devices, entries)), axis=0)
    sent, g_places, g_qkv = lax.optimization_barrier((sent, g_places, g_qkv))
    sent = swap(sent.reshape(devices, room, D)).reshape(-1, D)
    if by_kernel:
        g_own_places, first_grad = homecoming(
            g_places, g_qkv.reshape(-1, columns, D), owned, split, 3
        )
        mats_grad = jnp.where(me < QKV // columns, first_grad, rest_grad).T
    else:
        total = lax.psum(g_places.astype(F32), axis)
        spots = me * owned + jnp.arange(owned, dtype=jnp.int32) - VOCAB
        inside = (spots >= 0) & (spots < LENGTH)
        g_own_places = jnp.where(
            inside[:, None], total[jnp.clip(spots, 0, LENGTH - 1)], 0.0
        )
        mats_grad = lax.psum_scatter(
            jnp.concatenate([g_qkv, g_rest], axis=0), axis, scatter_dimension=0, tiled=True
        )
        mats_grad = mats_grad.astype(F32).T
    table_grad = dot_tn(pick(wanted, owned), sent) + g_own_places

    def send_more(state):
        turn, total = state
        key, asked = requests_of(chosen, owner, slot, owned, devices, room + turn * more, more)
        wanted = swap(asked.reshape(devices, more)).reshape(-1)
        sent = dot_tn(pick(key, devices * more), input_grad).astype(BF)
        sent = swap(sent.reshape(devices, more, D)).reshape(-1, D)
        return turn + 1, total + dot_tn(pick(wanted, owned), sent)

    _, table_grad = lax.while_loop(
        lambda state: state[0] < rounds, send_more, (jnp.int32(0), table_grad)
    )

    counter = jnp.float32(STEP)
    corr_one = 1.0 - jnp.power(jnp.float32(beta_one), counter)
    corr_two = 1.0 - jnp.power(jnp.float32(beta_two), counter)
    table_step, table_first_next = adam_direction(
        embed_table, table_first, table_second, table_grad, corr_one, corr_two, decay_rate
    )
    mats_step, mats_first_next = adam_direction(
        layer_mats, mats_first, mats_second, mats_grad, corr_one, corr_two, decay_rate
    )
    vecs_step, vecs_first_next = adam_direction(
        layer_vecs, vecs_first, vecs_second, vecs_grad, corr_one, corr_two, 0.0
    )
    return (
        outputs,
        input_grad,
        table_grad,
        mats_grad,
        vecs_grad,
        table_step,
        table_first_next,
        mats_step,
        mats_first_next,
        vecs_step,
        vecs_first_next,
    )


def solution(mesh):
    line = P("fsdp")
    by_rows = P("fsdp", None)
    by_cols = P(None, "fsdp")
    return jax.shard_map(
        functools.partial(body, mesh.shape["fsdp"]),
        mesh=mesh,
        in_specs=(
            line,
            line,
            line,
            line,
            by_rows,
            by_rows,
            by_rows,
            by_rows,
            by_cols,
            by_cols,
            by_cols,
            line,
            line,
            line,
        ),
        out_specs=(
            by_rows,
            by_rows,
            by_rows,
            by_cols,
            line,
            by_rows,
            by_rows,
            by_cols,
            by_cols,
            line,
            line,
        ),
        check_vma=False,
    )
```

profile of v0, /device:TPU:0, one launch (start us, length us, event | category | flops | bytes accessed | tf_op | source)
XLA Modules:
  0.0 560.5 jit_solution(14509856997746359085)
XLA Ops:
  7.2 2.1 convert_bitcast_fusion
  10.1 5.0 fusion.10
  15.1 4.4 convert_reduce_fusion
  20.8 2.2 select_reduce_fusion.2
  24.6 7.3 %all-to-all-start.4 = ((f32[32,1,337]{2,1,0:T(1,128)}), f32[32,1,337]{2,1,0:T(1,128)S(1)}, u32[]{:S(2)}, u32[]{:S(2)}) async-start(f32[32,1,337]{2,1,0:T(1,128)} %all_to_all.50), calls=%async_computation.4 | async-start | bytes 98304 | tf_op jit(solution)/shard_map/all_to_all | solution.py:1218
  32.0 7.4 %all-to-all-done.4 = f32[32,1,337]{2,1,0:T(1,128)S(1)} async-done(((f32[32,1,337]{2,1,0:T(1,128)}), f32[32,1,337]{2,1,0:T(1,128)S(1)}, u32[]{:S(2)}, u32[]{:S(2)}) %all-to-all-start.4) | async-done | bytes 43168 | tf_op jit(solution)/shard_map/all_to_all | solution.py:1218
  40.8 3.0 convolution_convert_fusion.1
  43.8 1.9 broadcast_in_dim.123
  46.3 3.5 all-to-all-start.5
  49.8 126.2 %share_places.1.place_ref = bf16[512,768]{1,0:T(8,128)(2,1)} custom-call(f32[472,768]{1,0:T(8,128)} %table_ref.1), custom_call_target="tpu_custom_call" | custom-call | bytes 60000000 | tf_op jit(solution)/shard_map/share_places/pallas_call | solution.py:678
  180.9 18.5 %entry.1 = (f32[2048,768]{1,0:T(8,128)}, bf16[2048,768]{1,0:T(8,128)(2,1)}, bf16[2048,2304]{1,0:T(8,128)(2,1)}) custom-call(s32[2048,1]{1,0:T(8,128)} %copy.37.key_ref, bf16[1536,768]{1,0:T(8,128)(2,1)} %bitcast.8.found_ref, bf16[2048,768]{1,0:T(8,128)(2,1)S(1)} %copy-done.11, bf16[512,768]{1,0:T(8,128)(2,1)} %share_places.1.place_ref, ...), custom_call_target="tpu_custom_call" | custom-call | flops 12999999488 | bytes 40000000 | tf_op jit(solution)/shard_map/entry/pallas_call | solution.py:286
  199.4 33.6 %attention_forward.1 = (bf16[2048,768]{1,0:T(8,128)(2,1)S(1)}, f32[24,2,512]{2,1,0:T(2,128)S(1)}) custom-call(bf16[2048,2304]{1,0:T(8,128)(2,1)} %get-tuple-element.220.q_ref.k_ref.v_ref, bf16[2048,2304]{1,0:T(8,128)(2,1)} %get-tuple-element.220.q_ref.k_ref.v_ref, bf16[2048,2304]{1,0:T(8,128)(2,1)} %get-tuple-element.220.q_ref.k_ref.v_ref), custom_call_target="tpu_custom_call" | custom-call | tf_op jit(solution)/shard_map/attention_forward/pallas_call | solution.py:78
  233.0 1.7 copy-done.1
  235.3 77.9 %middle.1 = (bf16[2048,768]{1,0:T(8,128)(2,1)}, bf16[2048,768]{1,0:T(8,128)(2,1)}, bf16[2048,3072]{1,0:T(8,128)(2,1)}, bf16[2048,768]{1,0:T(8,128)(2,1)}, bf16[2...) custom-call(bf16[2048,768]{1,0:T(8,128)(2,1)} %copy-done.1, ...), custom_call_target="tpu_custom_call" | custom-call | tf_op jit(solution)/shard_map/middle/pallas_call | solution.py:215
  315.1 43.1 %rest_gradients.1 = bf16[6912,768]{1,0:T(8,128)(2,1)} custom-call(bf16[2048,768]{1,0:T(8,128)(2,1)} %get-tuple-element.228.first_ref, bf16[2048,768]{1,0:T(8,128)(2,1)} %copy-done.1, bf16[2048,3072]{1,0:T(8,128)(2,1)} %get-tuple-element.229.up_ref, bf16[2048,768]{1,0:T(8,128)(2,1)} %get-tuple-element.230.normed_ref, ...), custom_call_target="tpu_custom_call" | custom-call | flops 22000001024 | bytes 50000000 | tf_op jit(solution)/shard_map/rest_gradients/pallas_call | solution.py:332
  358.2 81.9 %backward.1 = (bf16[2048,768]{1,0:T(8,128)(2,1)S(1)}, bf16[512,768]{1,0:T(8,128)(2,1)}, bf16[2304,768]{1,0:T(8,128)(2,1)}, f32[8,768]{1,0:T(8,128)}, f32[288,768]{1,0:T(8,128)}) custom-call(bf16[2048,2304]{1,0:T(8,128)(2,1)} %get-tuple-element.220.q_ref.k_ref.v_ref, bf16[2048,2304]{1,0:T(8,128)(2,1)} %get-tuple-element.220.q_ref.k_ref.v_ref, ...), custom_call_target="tpu_custom_call" | custom-call | flops 60000002048 | bytes 60000000 | tf_op jit(solution)/shard_map/backward/pallas_call | solution.py:1094
  441.8 10.0 %all-to-all-start.7 = ((f32[32,1,288]{2,1,0:T(1,128)}), f32[32,1,288]{2,1,0:T(1,128)}, u32[]{:S(2)}, u32[]{:S(2)}) async-start(f32[32,1,288]{2,1,0:T(1,128)} %all_to_all.55), calls=%async_computation.7 | async-start | bytes 98304 | tf_op jit(solution)/shard_map/all_to_all | solution.py:1218
  451.9 7.2 %fusion.13 = bf16[1536,768]{1,0:T(8,128)(2,1)} fusion(bf16[2048,768]{1,0:T(8,128)(2,1)S(1)} %get-tuple-element.479, s32[2048]{0:T(1024)S(1)} %get-tuple-element.297), kind=kOutput, calls=%fused_computation.30 | convolution fusion | flops 4836163584 | bytes 5513216 | tf_op jit(solution)/shard_map/dot_general | solution.py:49
  459.2 6.0 %all-to-all-start.6 = ((bf16[32,48,768]{2,1,0:T(8,128)(2,1)}), bf16[32,48,768]{2,1,0:T(8,128)(2,1)}, u32[]{:S(2)}, u32[]{:S(2)}) async-start(bf16[32,48,768]{2,1,0:T(8,128)(2,1)} %bitcast.57), calls=%async_computation.6 | async-start | bytes 4718592 | tf_op jit(solution)/shard_map/all_to_all | solution.py:1218
  466.3 72.0 %homecoming.1 = (f32[472,768]{1,0:T(8,128)S(1)}, f32[288,768]{1,0:T(8,128)S(1)}) custom-call(bf16[4,2,2,2,16,768]{5,4,3,2,1,0:T(8,128)(2,1)S(1)} %bitcast.54, bf16[8,288,768]{2,1,0:T(8,128)(2,1)S(1)} %bitcast.53), custom_call_target="tpu_custom_call" | custom-call | bytes 200000000 | tf_op jit(solution)/shard_map/homecoming/pallas_call | solution.py:938
  539.5 1.8 fusion.31
  542.8 3.3 fusion.24
  546.2 5.4 fusion.23
  551.6 1.7 copy.66
  (102 shorter events, 17.4 us)
Async XLA Ops:
  7.2 24.7 %copy-start.7 = (f32[472,768]{1,0:T(8,128)S(1)}, f32[472,768]{1,0:T(8,128)}, u32[]{:S(2)}) copy-start(f32[472,768]{1,0:T(8,128)} %table_ref.1) | copy-start | bytes 4349956
  7.2 173.7 %all-gather.2.cloned.1.call-start = ((), (), s32[]{:S(2)}) async-start(), calls=%async_computation.8 | async-start | bytes 14598144 | tf_op jit(solution)/shard_map/all_gather | solution.py:1220
  24.6 14.8 %all-to-all-start.4 = ((f32[32,1,337]{2,1,0:T(1,128)}), f32[32,1,337]{2,1,0:T(1,128)S(1)}, u32[]{:S(2)}, u32[]{:S(2)}) async-start(f32[32,1,337]{2,1,0:T(1,128)} %all_to_all.50), calls=%async_computation.4 | async-start | bytes 98304 | tf_op jit(solution)/shard_map/all_to_all | solution.py:1218
  40.8 3.0 copy-start.18
  45.7 131.7 %copy-start.17 = (s32[2048]{0:T(1024)S(1)}, s32[2048]{0:T(1024)}, u32[]{:S(2)}) copy-start(s32[2048]{0:T(1024)} %param.19) | copy-start | bytes 24580
  46.3 134.6 %all-to-all-start.5 = ((bf16[32,48,768]{2,1,0:T(8,128)(2,1)}), bf16[32,48,768]{2,1,0:T(8,128)(2,1)}, u32[]{:S(2)}, u32[]{:S(2)}) async-start(bf16[32,48,768]{2,1,0:T(8,128)(2,1)} %bitcast.7), calls=%async_computation.5 | async-start | bytes 4718592 | tf_op jit(solution)/shard_map/all_to_all | solution.py:1218
  49.8 131.1 %copy-start.11 = (bf16[2048,768]{1,0:T(8,128)(2,1)S(1)}, bf16[2048,768]{1,0:T(8,128)(2,1)}, u32[]{:S(2)}) copy-start(bf16[2048,768]{1,0:T(8,128)(2,1)} %get-tuple-element.219.extra_ref) | copy-start | bytes 9437188
  440.1 11.8 %copy-start.9 = (bf16[2048,768]{1,0:T(8,128)(2,1)}, bf16[2048,768]{1,0:T(8,128)(2,1)S(1)}, u32[]{:S(2)}) copy-start(bf16[2048,768]{1,0:T(8,128)(2,1)S(1)} %get-tuple-element.479) | copy-start | bytes 9437188
  441.8 17.4 %all-to-all-start.7 = ((f32[32,1,288]{2,1,0:T(1,128)}), f32[32,1,288]{2,1,0:T(1,128)}, u32[]{:S(2)}, u32[]{:S(2)}) async-start(f32[32,1,288]{2,1,0:T(1,128)} %all_to_all.55), calls=%async_computation.7 | async-start | bytes 98304 | tf_op jit(solution)/shard_map/all_to_all | solution.py:1218
  459.1 6.1 %copy-start = (bf16[2304,768]{1,0:T(8,128)(2,1)S(1)}, bf16[2304,768]{1,0:T(8,128)(2,1)}, u32[]{:S(2)}) copy-start(bf16[2304,768]{1,0:T(8,128)(2,1)} %get-tuple-element.238) | copy-start | bytes 10616836
  459.2 83.6 %all-to-all-start.6 = ((bf16[32,48,768]{2,1,0:T(8,128)(2,1)}), bf16[32,48,768]{2,1,0:T(8,128)(2,1)}, u32[]{:S(2)}, u32[]{:S(2)}) async-start(bf16[32,48,768]{2,1,0:T(8,128)(2,1)} %bitcast.57), calls=%async_computation.6 | async-start | bytes 4718592 | tf_op jit(solution)/shard_map/all_to_all | solution.py:1218
  466.3 73.1 %copy-start.8 = (f32[768,288]{0,1:T(8,128)S(1)}, f32[768,288]{0,1:T(8,128)}, u32[]{:S(2)}) copy-start(f32[768,288]{0,1:T(8,128)} %param.26) | copy-start | bytes 2654212
  466.3 73.1 %copy-start.14 = (f32[768,288]{0,1:T(8,128)S(1)}, f32[768,288]{0,1:T(8,128)}, u32[]{:S(2)}) copy-start(f32[768,288]{0,1:T(8,128)} %param.28) | copy-start | bytes 2654212
  466.3 73.1 %copy-start.15 = (f32[768,288]{0,1:T(8,128)S(1)}, f32[768,288]{0,1:T(8,128)}, u32[]{:S(2)}) copy-start(f32[768,288]{0,1:T(8,128)} %param.27) | copy-start | bytes 2654212
  466.3 73.1 %copy-start.16 = (f32[288,768]{1,0:T(8,128)S(1)}, f32[288,768]{1,0:T(8,128)}, u32[]{:S(2)}) copy-start(f32[288,768]{1,0:T(8,128)} %get-tuple-element.242) | copy-start | bytes 2654212
  539.4 2.7 copy-start.21
  539.5 2.7 copy-start.22
  539.5 2.7 copy-start.23
  539.5 3.3 copy-start.4
  539.5 3.3 copy-start.19
  542.2 4.0 copy-start.20
  542.8 3.4 copy-start.13
  546.2 5.4 copy-start.6
  546.2 5.4 copy-start.10
  (5 other events, 5.1 us)
Sparse Core Ops, SparseCore 0:
  11.5 144.8 all-gather.1
where the time goes:
time: 568 us; the launch traced here: 560 us
  Pallas kernels  453 us (80%)
  starting transfers between devices  26.8 us (5%)
  other arithmetic  25.1 us (4%)
  local copies, waits for them, and re-layouts  18.1 us (3%)
  between operations  16.2 us (3%)
  matrix products  13.5 us (2%)
  waiting for transfers between devices  7.5 us (1%)
    pallas_call x1, Pallas kernels, share_places(): pl.pallas_call(functools.partial(share_places_kernel, split), in_specs=[p...  126 us
    pallas_call x1, Pallas kernels, backward(): pl.pallas_call(functools.partial(backward_kernel, by_kernel), grid=(seqs,...  81.9 us
    pallas_call x1, Pallas kernels, middle(): pl.pallas_call(middle_kernel, grid=(rows // tile,), in_specs=[row(D), row...  77.9 us
    pallas_call x1, Pallas kernels, homecoming(): pl.pallas_call(functools.partial(homecoming_kernel, split), in_specs=[pl....  72 us
    pallas_call x1, Pallas kernels, rest_gradients(): pl.pallas_call(rest_kernel, grid=(1 + 2 * chunks,), in_specs=[full, full,...  43.1 us
    pallas_call x1, Pallas kernels, attention_forward(): pl.pallas_call(attention_forward_kernel, grid=(seqs, pairs), in_specs=[pl...  33.6 us
    all_to_all x4, starting transfers between devices, swap(): return lax.all_to_all(blocks, axis, 0, 0, tiled=True)  26.8 us
    pallas_call x1, Pallas kernels, entry(): pl.pallas_call(entry_kernel, grid=(rows // LENGTH,), in_specs=[row(1), fi...  18.5 us
  transfers between devices with their start and end apart: 5, of which 2 were waited for; matrix products, arithmetic and copies ran while one was open for 6% of the time, Pallas kernels for 35%

commit v1 on v0

--- a/solution.py
+++ b/solution.py
@@ -30,7 +30,6 @@
 MB = 1024 * 1024
 
 ROW_TILE = 256
-FF_TILE = 768
 
 
 def dot_nn(left, right):
@@ -49,51 +48,6 @@
     return lax.dot_general(
         left, right, (((0,), (0,)), ((), ())), preferred_element_type=F32
     )
-
-
-def attention_forward_kernel(q_ref, k_ref, v_ref, att_ref, lse_ref):
-    query = q_ref[...]
-    keys = k_ref[...]
-    values_t = v_ref[...].T
-    lane = lax.broadcasted_iota(jnp.int32, query.shape, 1)
-    outs = []
-    for half in range(2):
-        mine = (lane < HEAD_DIM) if half == 0 else (lane >= HEAD_DIM)
-        picked = jnp.where(mine, query, jnp.zeros_like(query))
-        scores = dot_nt(keys, picked)
-        highest = jnp.max(scores, 0, keepdims=True)
-        expo = jnp.exp2((scores - highest) * (SCORE * LOG2E))
-        total = jnp.sum(expo, 0, keepdims=True)
-        part = values_t[half * HEAD_DIM : (half + 1) * HEAD_DIM, :]
-        outs.append(dot_nn(part, expo.astype(BF)) / total)
-        lse_ref[0, half : half + 1, :] = highest * (SCORE * LOG2E) + jnp.log2(total)
-    att_ref[...] = jnp.concatenate(outs, 0).T.astype(BF)
-
-
-def attention_forward(projected):
-    rows = projected.shape[0]
-    seqs = rows // LENGTH
-    pairs = HEADS // 2
-    block = (LENGTH, 2 * HEAD_DIM)
-    return pl.pallas_call(
-        attention_forward_kernel,
-        grid=(seqs, pairs),
-        in_specs=[
-            pl.BlockSpec(block, lambda s, h: (s, h)),
-            pl.BlockSpec(block, lambda s, h: (s, pairs + h)),
-            pl.BlockSpec(block, lambda s, h: (s, 2 * pairs + h)),
-        ],
-        out_specs=[
-            pl.BlockSpec(block, lambda s, h: (s, h)),
-            pl.BlockSpec((1, 2, LENGTH), lambda s, h: (s * pairs + h, 0, 0)),
-        ],
-        out_shape=[
-            jax.ShapeDtypeStruct((rows, D), BF),
-            jax.ShapeDtypeStruct((seqs * pairs, 2, LENGTH), F32),
-        ],
-        compiler_params=pltpu.CompilerParams(vmem_limit_bytes=48 * MB),
-        name="attention_forward",
-    )(projected, projected, projected)
 
 
 def gelu_parts(values):
@@ -130,8 +84,14 @@
     go_ref,
     mask_ref,
     wout_ref,
-    wup_ref,
-    wdown_ref,
+    up_0,
+    up_1,
+    up_2,
+    up_3,
+    down_0,
+    down_1,
+    down_2,
+    down_3,
     vec_ref,
     bup_ref,
     out_ref,
@@ -149,6 +109,8 @@
     def _():
         sums_ref[...] = jnp.zeros_like(sums_ref)
 
+    ups = (up_0, up_1, up_2, up_3)
+    downs = (down_0, down_1, down_2, down_3)
     bias_out = vec_ref[0:1, :]
     gain_one = vec_ref[1:2, :]
     shift_one = vec_ref[2:3, :]
@@ -165,14 +127,14 @@
     normed_b = normed.astype(BF)
     normed_ref[...] = normed_b
     downward = jnp.zeros(normed.shape, F32)
-    for start in range(0, FF, FF_TILE):
-        cols = slice(start, start + FF_TILE)
-        upward = dot_nt(normed_b, wup_ref[cols, :]) + bup_ref[0:1, cols]
+    for start in range(0, FF, D):
+        cols = slice(start, start + D)
+        upward = dot_nt(normed_b, ups[start // D][...]) + bup_ref[0:1, cols]
         hidden, slope = gelu_parts(upward)
         slope_ref[:, cols] = slope
         hidden_b = hidden.astype(BF)
         hidden_ref[:, cols] = hidden_b
-        downward += dot_nn(hidden_b, wdown_ref[cols, :])
+        downward += dot_nn(hidden_b, downs[start // D][...])
     unit_two, scale_two = norm_parts(normed + downward + bias_down)
     out_ref[...] = (unit_two * gain_two + shift_two).astype(BF)
     g_out = go_ref[...].astype(F32) * mask_ref[...].astype(F32)
@@ -183,13 +145,13 @@
     g_mid_b = g_mid.astype(BF)
     gmid_ref[...] = g_mid_b
     g_normed = g_mid
-    for start in range(0, FF, FF_TILE):
-        cols = slice(start, start + FF_TILE)
-        g_up = dot_nt(g_mid_b, wdown_ref[cols, :]) * slope_ref[:, cols]
+    for start in range(0, FF, D):
+        cols = slice(start, start + D)
+        g_up = dot_nt(g_mid_b, downs[start // D][...]) * slope_ref[:, cols]
         sums_ref[0:1, cols] += jnp.sum(g_up, 0, keepdims=True)
         g_up_b = g_up.astype(BF)
         gup_ref[:, cols] = g_up_b
-        g_normed += dot_nn(g_up_b, wup_ref[cols, :])
+        g_normed += dot_nn(g_up_b, ups[start // D][...])
     note(2, g_normed * unit_one)
     note(3, g_normed)
     g_first = norm_back(g_normed * gain_one, unit_one, scale_one)
@@ -200,7 +162,7 @@
     gatt_ref[...] = dot_nn(g_first_b, wout_ref[...]).astype(BF)
 
 
-def middle(attended, inputs, out_grad, masked, mats_t, vecs, bias_up):
+def middle(attended, inputs, out_grad, masked, rest, vecs, bias_up):
     rows = attended.shape[0]
     tile = ROW_TILE
 
@@ -220,9 +182,7 @@
             row(D),
             row(D),
             row(1),
-            whole((D, D), 3),
-            whole((FF, D), 1),
-            whole((FF, D), 2),
+            *[whole((D, D), place) for place in range(9)],
             whole((8, D)),
             whole((1, FF)),
         ],
@@ -251,61 +211,13 @@
         scratch_shapes=[pltpu.VMEM((tile, FF), F32)],
         compiler_params=pltpu.CompilerParams(vmem_limit_bytes=56 * MB),
         name="middle",
-    )(attended, inputs, out_grad, masked, mats_t, mats_t, mats_t, vecs, bias_up)
-
-
-def entry_kernel(
-    key_ref, found_ref, extra_ref, place_ref, w_ref, bias_ref, x_ref, xb_ref, proj_ref
-):
-    slots = lax.broadcasted_iota(jnp.int32, (LENGTH, found_ref.shape[0]), 1)
-    picked = (key_ref[...] == slots).astype(BF)
-    inputs = dot_nn(picked, found_ref[...]) + extra_ref[...].astype(F32)
-    inputs = inputs + place_ref[...].astype(F32)
-    x_ref[...] = inputs
-    inputs_b = inputs.astype(BF)
-    xb_ref[...] = inputs_b
-    for start in range(0, QKV, D):
-        cols = slice(start, start + D)
-        part = dot_nt(inputs_b, w_ref[cols, :]) + bias_ref[:, cols]
-        proj_ref[:, cols] = part.astype(BF)
+    )(attended, inputs, out_grad, masked, *[rest] * 9, vecs, bias_up)
 
 
 def fixed(shape, place=0):
     return pl.BlockSpec(
         shape, lambda i: (place, 0), pipeline_mode=pl.Buffered(buffer_count=1)
     )
-
-
-def entry(key, found, extra, places, mats_t, bias):
-    rows = key.shape[0]
-    slots = found.shape[0]
-
-    def row(width):
-        return pl.BlockSpec((LENGTH, width), lambda i: (i, 0))
-
-    return pl.pallas_call(
-        entry_kernel,
-        grid=(rows // LENGTH,),
-        in_specs=[
-            row(1),
-            fixed((slots, D)),
-            row(D),
-            fixed((LENGTH, D)),
-            fixed((QKV, D)),
-            fixed((1, QKV)),
-        ],
-        out_specs=[row(D), row(D), row(QKV)],
-        out_shape=[
-            jax.ShapeDtypeStruct((rows, D), F32),
-            jax.ShapeDtypeStruct((rows, D), BF),
-            jax.ShapeDtypeStruct((rows, QKV), BF),
-        ],
-        compiler_params=pltpu.CompilerParams(vmem_limit_bytes=56 * MB),
-        cost_estimate=pl.CostEstimate(
-            flops=13_000_000_000, bytes_accessed=40_000_000, transcendentals=0
-        ),
-        name="entry",
-    )(key[:, None], found, extra, places, mats_t, bias)
 
 
 def rest_kernel(first_ref, att_ref, up_ref, normed_ref, hidden_ref, mid_ref, out_ref):
@@ -391,6 +303,153 @@
     pl.semaphore_wait(barrier, jnp.where(inner, 5, 4))
 
 
+class RestSpread:
+    def __init__(self, in_ref, out_ref, scratch):
+        self.in_ref, self.out_ref = in_ref, out_ref
+        self.own_sem, self.send_sem, self.recv_sem = scratch
+        self.place = neighbours()
+
+    @staticmethod
+    def scratch():
+        return [
+            pltpu.SemaphoreType.DMA,
+            pltpu.SemaphoreType.DMA((5, 24)),
+            pltpu.SemaphoreType.DMA((24,)),
+        ]
+
+    def copy(self, shard, device, kind, source=None):
+        return pltpu.make_async_remote_copy(
+            src_ref=self.out_ref.at[shard] if source is None else source,
+            dst_ref=self.out_ref.at[shard],
+            send_sem=self.send_sem.at[kind, shard],
+            recv_sem=self.recv_sem.at[shard],
+            device_id=(device,),
+            device_id_type=MESH,
+        )
+
+    def shard(self, plane, other_a, other_b):
+        me, core, z, a, b, step_a, step_b, near_a, near_b, twin = self.place
+        a_at = 1 - a if other_a else a
+        b_at = 1 - b if other_b else b
+        return jnp.maximum(plane - 1, 0) * 8 + a_at * step_a + b_at * step_b + core
+
+    def planes(self, far):
+        z = self.place[2]
+        for way in (1, -1) if far else (1,):
+            plane = z - way * far
+            yield way, plane, jnp.logical_and(plane >= 1, plane < PLANES)
+
+    def routes(self, far):
+        me, core, z, a, b, step_a, step_b, near_a, near_b, twin = self.place
+        for way, plane, there in self.planes(far):
+            shard = self.shard(plane, False, False)
+            for onward in (way,) if far else (1, -1):
+                goes = jnp.logical_and(z + onward >= 0, z + onward < PLANES)
+                yield (
+                    jnp.logical_and(there, goes),
+                    shard,
+                    me + 8 * onward,
+                    0 if onward == 1 else 1,
+                )
+            yield there, shard, near_b, 3
+            yield there, shard, near_a, 2
+            yield there, shard, twin, 4
+
+    def routes_a(self, far):
+        near_b, twin = self.place[8:]
+        for way, plane, there in self.planes(far):
+            shard = self.shard(plane, True, False)
+            yield there, shard, near_b, 3
+            yield there, shard, twin, 4
+
+    def routes_b(self, far):
+        twin = self.place[9]
+        for way, plane, there in self.planes(far):
+            for other_a in (False, True):
+                yield there, self.shard(plane, other_a, True), twin, 4
+
+    def own(self):
+        return pltpu.make_async_copy(
+            self.in_ref, self.out_ref.at[self.shard(self.place[2], False, False)], self.own_sem
+        )
+
+    def start(self):
+        me, core, z, a, b, step_a, step_b, near_a, near_b, twin = self.place
+        greet(me, z, near_a, near_b, twin)
+
+        @pl.when(z > 0)
+        def _():
+            self.own().start()
+
+        for goes, shard, device, kind in self.routes(0):
+            pl.when(goes)(
+                lambda shard=shard, device=device, kind=kind: self.copy(
+                    shard, device, kind, self.in_ref
+                ).start()
+            )
+
+    def pass_on(self, routes):
+        seen = []
+        for goes, shard, device, kind in routes:
+            if kind == 4:
+                seen.append((goes, shard))
+        for goes, shard in seen:
+            pl.when(goes)(
+                lambda shard=shard: self.copy(shard, self.place[9], 4).wait_recv()
+            )
+            for other, place, device, kind in routes:
+                if place is shard:
+                    pl.when(other)(
+                        lambda shard=shard, device=device, kind=kind: self.copy(
+                            shard, device, kind
+                        ).start()
+                    )
+
+    def column(self, far):
+        self.pass_on(list(self.routes(far)))
+
+    def along_a(self, far):
+        self.pass_on(list(self.routes_a(far)))
+
+    def along_b(self, far):
+        self.pass_on(list(self.routes_b(far)))
+
+    def end(self):
+        me, core, z, a, b, step_a, step_b, near_a, near_b, twin = self.place
+
+        def from_twin(place, carry):
+            self.copy(place * 2 + 1 - core, twin, 4).wait_recv()
+            return carry
+
+        lax.fori_loop(0, 12, from_twin, 0)
+        for far in range(PLANES):
+            for routes in (self.routes(far), self.routes_a(far), self.routes_b(far)):
+                for goes, shard, device, kind in routes:
+                    pl.when(goes)(
+                        lambda shard=shard, device=device, kind=kind: self.copy(
+                            shard, device, kind
+                        ).wait_send()
+                    )
+
+        @pl.when(z > 0)
+        def _():
+            self.own().wait()
+
+    def schedule(self):
+        return {
+            0: [self.start],
+            4: [lambda: self.along_a(0)],
+            5: [lambda: self.column(1)],
+            8: [lambda: self.along_a(1), lambda: self.along_b(0)],
+            11: [lambda: self.column(2)],
+            13: [lambda: self.along_a(2), lambda: self.along_b(1)],
+            16: [lambda: self.column(3)],
+            18: [lambda: self.along_a(3), lambda: self.along_b(2)],
+            24: [lambda: self.along_b(3)],
+            27: [self.end],
+        }
+
+
 class RestSums:
     TURNS = PLANES - 1
 
@@ -588,13 +647,28 @@
 
 
 PIECES = 4
-
-
-def share_places_kernel(split, table_ref, out_ref, stage, load_sem, send_sem, recv_sem):
+CHUNKS = 3
+
+
+def broadcast_kernel(
+    split,
+    table_ref,
+    block_ref,
+    out_ref,
+    w_ref,
+    stage,
+    own_sem,
+    load_sem,
+    send_sem,
+    recv_sem,
+    w_send,
+    w_recv,
+):
     first_owner, first_row, count = split
     me, core, z, a, b, step_a, step_b, near_a, near_b, twin = neighbours()
     greet(me, z, near_a, near_b, twin)
     rows = LENGTH // PIECES
+    height = block_ref.shape[0] // CHUNKS
     root = first_owner + 1
     gift = pltpu.make_async_remote_copy(
         src_ref=table_ref.at[pl.ds(first_row, count)],
@@ -609,6 +683,8 @@
         stage.at[pl.ds(count, LENGTH - count)],
         load_sem.at[2],
     )
+    shard = lax.rem(me, 8)
+    own = pltpu.make_async_copy(block_ref, w_ref.at[shard], own_sem)
 
     @pl.when(me == first_owner)
     def _():
@@ -617,8 +693,10 @@
     @pl.when(me == root)
     def _():
         mine.start()
-        mine.wait()
-        gift.wait_recv()
+
+    @pl.when(z == 0)
+    def _():
+        own.start()
 
     def copy(piece, device, kind):
         part = pl.ds(piece * rows, rows)
@@ -631,6 +709,17 @@
             device_id_type=MESH,
         )
 
+    def block(place, chunk, device, kind, source=None):
+        part = pl.ds(chunk * height, height)
+        return pltpu.make_async_remote_copy(
+            src_ref=w_ref.at[place, part] if source is None else source.at[part],
+            dst_ref=w_ref.at[place, part],
+            send_sem=w_send.at[kind, place, chunk],
+            recv_sem=w_recv.at[place, chunk],
+            device_id=(device,),
+            device_id_type=MESH,
+        )
+
     trunk = jnp.logical_and(core == 1, jnp.logical_and(a == 1, b == 1))
     branch = jnp.logical_and(core == 1, jnp.logical_and(a == 0, b == 1))
     routes = (
@@ -639,33 +728,103 @@
         (jnp.logical_or(trunk, branch), near_b),
         (core == 1, twin),
     )
-    for piece in range(PIECES):
+    shard_a = (1 - a) * step_a + b * step_b + core
+    shards_b = [
+        a * step_a + (1 - b) * step_b + core,
+        (1 - a) * step_a + (1 - b) * step_b + core,
+    ]
+
+    def from_own(chunk):
+        def sends(source):
+            pl.when(z < PLANES - 1)(lambda: block(shard, chunk, me + 8, 0, source).start())
+            block(shard, chunk, near_b, 1, source).start()
+            block(shard, chunk, near_a, 2, source).start()
+            block(shard, chunk, twin, 3, source).start()
+
+        @pl.when(z == 0)
+        def _():
+            sends(block_ref)
+
+        @pl.when(z > 0)
+        def _():
+            block(shard, chunk, twin, 3).wait_recv()
+            sends(None)
+
+    def from_a(chunk):
+        block(shard_a, chunk, twin, 3).wait_recv()
+        block(shard_a, chunk, near_b, 1).start()
+        block(shard_a, chunk, twin, 3).start()
+
+    def from_b(chunk):
+        for place in shards_b:
+            block(place, chunk, twin, 3).wait_recv()
+            block(place, chunk, twin, 3).start()
+
+    def positions(piece):
         part = slice(piece * rows, (piece + 1) * rows)
 
         @pl.when(me == root)
-        def _(part=part):
+        def _():
+            if piece == 0:
+                mine.wait()
+                gift.wait_recv()
             out_ref[part, :] = stage[part, :].astype(BF)
 
         @pl.when(me != root)
-        def _(piece=piece):
+        def _():
             copy(piece, twin, 3).wait_recv()
 
         for kind, (goes, device) in enumerate(routes):
-
-            @pl.when(goes)
-            def _(piece=piece, device=device, kind=kind):
-                copy(piece, device, kind).start()
-
+            pl.when(goes)(lambda kind=kind, device=device: copy(piece, device, kind).start())
+
+    from_own(0)
+    positions(0)
+    from_own(1)
+    from_a(0)
+    positions(1)
+    from_own(2)
+    from_a(1)
+    from_b(0)
+    positions(2)
+    from_a(2)
+    from_b(1)
+    positions(3)
+    from_b(2)
+
+    def from_twin(place, carry):
+        for chunk in range(CHUNKS):
+            block(place * 2 + 1 - core, chunk, twin, 3).wait_recv()
+        return carry
+
+    lax.fori_loop(0, 4, from_twin, 0)
     for piece in range(PIECES):
         for kind, (goes, device) in enumerate(routes):
-
-            @pl.when(goes)
-            def _(piece=piece, device=device, kind=kind):
-                copy(piece, device, kind).wait_send()
+            pl.when(goes)(
+                lambda piece=piece, kind=kind, device=device: copy(
+                    piece, device, kind
+                ).wait_send()
+            )
+    for chunk in range(CHUNKS):
+
+        @pl.when(z < PLANES - 1)
+        def _(chunk=chunk):
+            block(shard, chunk, me + 8, 0).wait_send()
+
+        block(shard, chunk, near_b, 1).wait_send()
+        block(shard, chunk, near_a, 2).wait_send()
+        block(shard, chunk, twin, 3).wait_send()
+        block(shard_a, chunk, near_b, 1).wait_send()
+        block(shard_a, chunk, twin, 3).wait_send()
+        for place in shards_b:
+            block(place, chunk, twin, 3).wait_send()
 
     @pl.when(me == first_owner)
     def _():
         gift.wait_send()
+
+    @pl.when(z == 0)
+    def _():
+        own.wait()
 
 
 def place_split(devices, owned):
@@ -674,25 +833,31 @@
     return first_owner, first_row, owned - first_row
 
 
-def share_places(table, split, ident):
+def broadcast(table, block, split, ident):
     return pl.pallas_call(
-        functools.partial(share_places_kernel, split),
-        in_specs=[pl.BlockSpec(memory_space=pl.ANY)],
-        out_specs=pl.BlockSpec(memory_space=pltpu.VMEM),
-        out_shape=jax.ShapeDtypeStruct((LENGTH, D), BF),
+        functools.partial(broadcast_kernel, split),
+        in_specs=[pl.BlockSpec(memory_space=pl.ANY)] * 2,
+        out_specs=[
+            pl.BlockSpec(memory_space=pltpu.VMEM),
+            pl.BlockSpec(memory_space=pl.ANY),
+        ],
+        out_shape=[
+            jax.ShapeDtypeStruct((LENGTH, D), BF),
+            jax.ShapeDtypeStruct((8,) + block.shape, BF),
+        ],
         scratch_shapes=[
             pltpu.VMEM((LENGTH, D), F32),
+            pltpu.SemaphoreType.DMA,
             pltpu.SemaphoreType.DMA((3,)),
             pltpu.SemaphoreType.DMA((4, PIECES)),
             pltpu.SemaphoreType.DMA((PIECES,)),
+            pltpu.SemaphoreType.DMA((4, 8, CHUNKS)),
+            pltpu.SemaphoreType.DMA((8, CHUNKS)),
         ],
         compiler_params=pltpu.CompilerParams(collective_id=ident, has_side_effects=True),
-        cost_estimate=pl.CostEstimate(flops=0, bytes_accessed=60_000_000, transcendentals=0),
-        name="share_places",
-    )(table)
-
-
-CHUNKS = 3
+        cost_estimate=pl.CostEstimate(flops=0, bytes_accessed=100_000_000, transcendentals=0),
+        name="broadcast",
+    )(table, block)
 
 
 def homecoming_kernel(
@@ -978,6 +1143,130 @@
     )(place_sums.reshape((4, 2, 2, 2) + small), first)
 
 
+def forward_kernel(
+    by_kernel,
+    key_ref,
+    found_ref,
+    extra_ref,
+    place_ref,
+    w_ref,
+    bias_ref,
+    block_ref,
+    x_ref,
+    xb_ref,
+    proj_ref,
+    att_ref,
+    lse_ref,
+    *scratch,
+):
+    seq, head = pl.program_id(0), pl.program_id(1)
+    pairs = HEADS // 2
+    step = seq * (pairs + 1) + head
+    if by_kernel:
+        gather = RestSpread(block_ref, scratch[0], scratch[1:])
+        for when, actions in gather.schedule().items():
+
+            @pl.when(step == when)
+            def _(actions=actions):
+                for action in actions:
+                    action()
+
+    @pl.when(head == 0)
+    def _():
+        slots = lax.broadcasted_iota(jnp.int32, (LENGTH, found_ref.shape[0]), 1)
+        picked = (key_ref[...] == slots).astype(BF)
+        inputs = dot_nn(picked, found_ref[...]) + extra_ref[...].astype(F32)
+        inputs = inputs + place_ref[...].astype(F32)
+        x_ref[...] = inputs
+        inputs_b = inputs.astype(BF)
+        xb_ref[...] = inputs_b
+        for start in range(0, QKV, D):
+            cols = slice(start, start + D)
+            part = dot_nt(inputs_b, w_ref[cols, :]) + bias_ref[:, cols]
+            proj_ref[:, cols] = part.astype(BF)
+
+    @pl.when(head > 0)
+    def _():
+        width = 2 * HEAD_DIM
+        start = (head - 1) * width
+        query = proj_ref[:, pl.ds(pl.multiple_of(start, width), width)]
+        keys = proj_ref[:, pl.ds(pl.multiple_of(D + start, width), width)]
+        values_t = proj_ref[:, pl.ds(pl.multiple_of(2 * D + start, width), width)].T
+        lane = lax.broadcasted_iota(jnp.int32, query.shape, 1)
+        outs = []
+        for half in range(2):
+            mine = (lane < HEAD_DIM) if half == 0 else (lane >= HEAD_DIM)
+            picked = jnp.where(mine, query, jnp.zeros_like(query))
+            scores = dot_nt(keys, picked)
+            highest = jnp.max(scores, 0, keepdims=True)
+            expo = jnp.exp2((scores - highest) * (SCORE * LOG2E))
+            total = jnp.sum(expo, 0, keepdims=True)
+            part = values_t[half * HEAD_DIM : (half + 1) * HEAD_DIM, :]
+            outs.append(dot_nn(part, expo.astype(BF)) / total)
+            lse_ref[0, half : half + 1, :] = highest * (SCORE * LOG2E) + jnp.log2(total)
+        att_ref[...] = jnp.concatenate(outs, 0).T.astype(BF)
+
+
+def forward(by_kernel, key, found, extra, places, w_qkv, bias, block, ident):
+    rows = key.shape[0]
+    seqs = rows // LENGTH
+    pairs = HEADS // 2
+    slots = found.shape[0]
+
+    def row(width):
+        return pl.BlockSpec((LENGTH, width), lambda s, h: (s, 0))
+
+    def steady(shape):
+        return pl.BlockSpec(
+            shape, lambda s, h: (0, 0), pipeline_mode=pl.Buffered(buffer_count=1)
+        )
+
+    out_specs = [
+        row(D),
+        row(D),
+        row(QKV),
+        pl.BlockSpec((LENGTH, 2 * HEAD_DIM), lambda s, h: (s, jnp.maximum(h - 1, 0))),
+        pl.BlockSpec(
+            (1, 2, LENGTH), lambda s, h: (s * pairs + jnp.maximum(h - 1, 0), 0, 0)
+        ),
+    ]
+    out_shape = [
+        jax.ShapeDtypeStruct((rows, D), F32),
+        jax.ShapeDtypeStruct((rows, D), BF),
+        jax.ShapeDtypeStruct((rows, QKV), BF),
+        jax.ShapeDtypeStruct((rows, D), BF),
+        jax.ShapeDtypeStruct((seqs * pairs, 2, LENGTH), F32),
+    ]
+    params = {}
+    scratch = []
+    if by_kernel:
+        out_specs.append(pl.BlockSpec(memory_space=pl.ANY))
+        out_shape.append(jax.ShapeDtypeStruct((24,) + block.shape, BF))
+        params = dict(collective_id=ident, has_side_effects=True)
+        scratch = RestSpread.scratch()
+    return pl.pallas_call(
+        functools.partial(forward_kernel, by_kernel),
+        grid=(seqs, pairs + 1),
+        in_specs=[
+            row(1),
+            steady((slots, D)),
+            row(D),
+            steady((LENGTH, D)),
+            steady((QKV, D)),
+            steady((1, QKV)),
+            pl.BlockSpec(memory_space=pl.ANY),
+        ],
+        out_specs=out_specs,
+        out_shape=out_shape,
+        scratch_shapes=scratch,
+        compiler_params=pltpu.CompilerParams(vmem_limit_bytes=56 * MB, **params),
+        cost_estimate=pl.CostEstimate(
+            flops=40_000_000_000, bytes_accessed=60_000_000, transcendentals=0
+        ),
+        name="forward",
+    )(key[:, None], found, extra, places, w_qkv, bias, block)
+
+
 def backward_kernel(
     by_kernel,
     q_ref,
@@ -1070,7 +1359,7 @@
         place_ref[...] = places[...].astype(BF)
 
 
-def backward(by_kernel, projected, attended, grad_att, lse, g_first, inputs_b, mats_t, rest, ident):
+def backward(by_kernel, projected, attended, grad_att, lse, g_first, inputs_b, w_qkv, rest, ident):
     rows = projected.shape[0]
     seqs = rows // LENGTH
     pairs = HEADS // 2
@@ -1145,7 +1434,7 @@
         lse,
         g_first,
         inputs_b,
-        mats_t,
+        w_qkv,
         rest,
     )
 
@@ -1217,7 +1506,7 @@
     def swap(blocks):
         return lax.all_to_all(blocks, axis, 0, 0, tiled=True)
 
-    mats_t = lax.all_gather(layer_mats.astype(BF).T, axis, axis=0, tiled=True)
+    block = layer_mats.astype(BF).T
 
     room = 16 * -(-1536 // (16 * devices))
     more = 16
@@ -1225,11 +1514,13 @@
     slot = slots_of(chosen, owned)
     most = jnp.max(slot) + 1
     key, asked = requests_of(chosen, owner, slot, owned, devices, 0, room)
+    _, asked_more = requests_of(chosen, owner, slot, owned, devices, room, more)
     table_b = embed_table.astype(BF)
     own_vecs = layer_vecs.astype(BF).astype(F32)
     notes = jnp.concatenate(
         [
             asked.reshape(devices, room).astype(F32),
+            asked_more.reshape(devices, more).astype(F32),
             jnp.broadcast_to(own_vecs[None], (devices, entries)),
             jnp.broadcast_to(most.astype(F32), (devices, 1)),
         ],
@@ -1237,27 +1528,42 @@
     )
     notes = swap(notes)
     wanted = notes[:, :room].astype(jnp.int32).reshape(-1)
-    vecs = notes[:, room : room + entries].reshape(-1)
-    longest = jnp.max(notes[:, room + entries]).astype(jnp.int32)
+    wanted_more = notes[:, room : room + more].astype(jnp.int32).reshape(-1)
+    vecs = notes[:, room + more : room + more + entries].reshape(-1)
+    longest = jnp.max(notes[:, room + more + entries]).astype(jnp.int32)
     found = dot_nn(pick(wanted, owned), table_b).astype(BF)
     found = swap(found.reshape(devices, room, D)).reshape(-1, D)
     if by_kernel:
-        places = share_places(embed_table, split, 1)
+        places, w_qkv = broadcast(embed_table, block, split, 1)
+        w_qkv = w_qkv.reshape(QKV, D)
     else:
         spots = VOCAB + jnp.arange(LENGTH, dtype=jnp.int32) - me * owned
         places = lax.psum(dot_nn(pick(spots, owned), table_b), axis).astype(BF)
+        mats_t = lax.all_gather(block, axis, axis=0, tiled=True)
+        w_qkv, rest = mats_t[:QKV], mats_t[QKV:]
     rounds = (longest - room + more - 1) // more
+
+    def further(turn):
+        key, asked = requests_of(chosen, owner, slot, owned, devices, room + turn * more, more)
+        wanted = lax.cond(
+            turn == 0,
+            lambda: wanted_more,
+            lambda: swap(asked.reshape(devices, more)).reshape(-1),
+        )
+        return key, wanted
 
     def fetch_more(state):
         turn, extra = state
-        key, asked = requests_of(chosen, owner, slot, owned, devices, room + turn * more, more)
-        wanted = swap(asked.reshape(devices, more)).reshape(-1)
+        key, wanted = further(turn)
         found = dot_nn(pick(wanted, owned), table_b).astype(BF)
         found = swap(found.reshape(devices, more, D)).reshape(-1, D)
         return turn + 1, extra + dot_nn(pick(key, devices * more), found).astype(BF)
 
+    nothing, places = lax.optimization_barrier((jnp.zeros((), BF), places))
     _, extra = lax.while_loop(
-        lambda state: state[0] < rounds, fetch_more, (jnp.int32(0), jnp.zeros((rows, D), BF))
+        lambda state: state[0] < rounds,
+        fetch_more,
+        (jnp.int32(0), jnp.broadcast_to(nothing, (rows, D))),
     )
 
     bias_qkv = jnp.concatenate([vecs[:D], jnp.zeros((D,), F32), vecs[D : 2 * D]])[None]
@@ -1266,8 +1572,10 @@
         [vecs[2 * D : 5 * D], vecs[5 * D + FF :], jnp.zeros((2 * D,), F32)]
     ).reshape(8, D)
 
-    inputs, inputs_b, projected = entry(key, found, extra, places, mats_t, bias_qkv)
-    attended, lse = attention_forward(projected)
+    results = forward(by_kernel, key, found, extra, places, w_qkv, bias_qkv, block, 4)
+    inputs, inputs_b, projected, attended, lse = results[:5]
+    if by_kernel:
+        rest = results[5].reshape(-1, D)
     (
         outputs,
         normed_b,
@@ -1278,7 +1586,7 @@
         g_first_b,
         g_att_b,
         sums,
-    ) = middle(attended, inputs, out_grad, masked[:, None], mats_t, small, bias_up)
+    ) = middle(attended, inputs, out_grad, masked[:, None], rest, small, bias_up)
     g_rest = rest_gradients(g_first_b, attended, g_up_b, normed_b, hidden_b, g_mid_b)
     input_grad, g_places, g_qkv, bias_sums, rest_grad = backward(
         by_kernel,
@@ -1288,7 +1596,7 @@
         lse,
         g_first,
         inputs_b,
-        mats_t,
+        w_qkv,
         g_rest.reshape(-1, columns, D),
         2,
     )
@@ -1330,8 +1638,7 @@
 
     def send_more(state):
         turn, total = state
-        key, asked = requests_of(chosen, owner, slot, owned, devices, room + turn * more, more)
-        wanted = swap(asked.reshape(devices, more)).reshape(-1)
+        key, wanted = further(turn)
         sent = dot_tn(pick(key, devices * more), input_grad).astype(BF)
         sent = swap(sent.reshape(devices, more, D)).reshape(-1, D)
         return turn + 1, total + dot_tn(pick(wanted, owned), sent)

time: 568 us -> 652 us (1.15)
  waiting for transfers between devices: 7.5 us -> 90.9 us
  starting transfers between devices: 26.8 us -> 46.2 us
  Pallas kernels: 453 us -> 437 us
  between operations: 16.2 us -> 2.67 us
  matrix products: 13.5 us -> 25.7 us
    all_to_all x4 -> x6, waiting for transfers between devices: 7.48 us -> 90.9 us  [swap(): return lax.all_to_all(blocks, axis, 0, 0, tiled=True)]
    all_to_all x4 -> x6, starting transfers between devices: 26.8 us -> 46.2 us  [swap(): return lax.all_to_all(blocks, axis, 0, 0, tiled=True)]
    pallas_call x1, Pallas kernels: 43.1 us -> 32.1 us  [rest_gradients(): pl.pallas_call(rest_kernel, grid=(1 + 2 * chunks,), in_specs=[full, full,...]
    pallas_call x3 -> x2, Pallas kernels: 178 us -> 172 us  [the longest x1 92.5 us: broadcast(): pl.pallas_call(functools.partial(broadcast_kernel, split), in_specs=[pl.B...]
    dot_general x2 -> x4, matrix products: 10.6 us -> 16.4 us  [dot_tn(): lax.dot_general(left, right, (((0,), (0,)), ((), ())), preferred_element_...]
  transfers between devices with their start and end apart: 5 -> 6, of which waited for: 2 -> 4; matrix products, arithmetic and copies ran while one was open for 6% -> 3% of each run, Pallas kernels for 35% -> 25%
where the time goes in v1:
time: 652 us; the launch traced here: 649 us
  Pallas kernels  437 us (67%)
  waiting for transfers between devices  90.9 us (14%)
  starting transfers between devices  46.2 us (7%)
  other arithmetic  29.2 us (4%)
  matrix products  25.7 us (4%)
  local copies, waits for them, and re-layouts  17.1 us (3%)
    pallas_call x1, Pallas kernels, broadcast(): pl.pallas_call(functools.partial(broadcast_kernel, split), in_specs=[pl.B...  92.5 us
    all_to_all x6, waiting for transfers between devices, swap(): return lax.all_to_all(blocks, axis, 0, 0, tiled=True)  90.9 us
    pallas_call x1, Pallas kernels, backward(): pl.pallas_call(functools.partial(backward_kernel, by_kernel), grid=(seqs,...  82.4 us
    pallas_call x1, Pallas kernels, forward(): pl.pallas_call(functools.partial(forward_kernel, by_kernel), grid=(seqs,...  79.7 us
    pallas_call x1, Pallas kernels, middle(): pl.pallas_call(middle_kernel, grid=(rows // tile,), in_specs=[row(D), row...  78 us
    pallas_call x1, Pallas kernels, homecoming(): pl.pallas_call(functools.partial(homecoming_kernel, split), in_specs=[pl....  72 us
    all_to_all x6, starting transfers between devices, swap(): return lax.all_to_all(blocks, axis, 0, 0, tiled=True)  46.2 us
    pallas_call x1, Pallas kernels, rest_gradients(): pl.pallas_call(rest_kernel, grid=(1 + 2 * chunks,), in_specs=[full, full,...  32.1 us
  transfers between devices with their start and end apart: 6, of which 4 were waited for; matrix products, arithmetic and copies ran while one was open for 3% of the time, Pallas kernels for 25%

profile of v1, /device:TPU:0, one launch (start us, length us, event | category | flops | bytes accessed | tf_op | source)
XLA Modules:
  0.0 648.6 jit_solution(7940535315584131870)
XLA Ops:
  1.4 5.0 fusion.4
  6.4 4.4 convert_reduce_fusion
  17.2 7.3 %all-to-all-start.4 = ((f32[32,1,353]{2,1,0:T(1,128)}), f32[32,1,353]{2,1,0:T(1,128)S(1)}, u32[]{:S(2)}, u32[]{:S(2)}) async-start(f32[32,1,353]{2,1,0:T(1,128)} %all_to_all.44), calls=%async_computation.4 | async-start | bytes 98304 | tf_op jit(solution)/shard_map/all_to_all | solution.py:1507
  28.0 92.5 %broadcast.172 = (bf16[512,768]{1,0:T(8,128)(2,1)}, bf16[8,288,768]{2,1,0:T(8,128)(2,1)}) custom-call(f32[472,768]{1,0:T(8,128)} %table_ref.1, bf16[288,768]{1,0:T(8,128)(2,1)} %convert_bitcast_fusion.block_ref), custom_call_target="tpu_custom_call" | custom-call | bytes 100000000 | tf_op jit(solution)/shard_map/broadcast/pallas_call | solution.py:837
  122.1 3.0 convolution_convert_fusion.3
  127.0 30.4 %while.24 = (s32[]{:T(128)}, bf16[2048,768]{1,0:T(8,128)(2,1)}, s32[]{:T(128)}, s32[2048]{0:T(1024)S(1)}, s32[2048]{0:T(1024)S(1)}, /*index=5*/s32[2048]{0:T(102...) while((s32[]{:T(128)}, bf16[2048,768]{1,0:T(8,128)(2,1)}, ...), condition=%wide.region_10.11_spmd, body=%wide.region_6.10_spmd.sunk | while | flops 1989801472 | bytes 13140227 | solution.py:1563
  131.9 20.6 %all-to-all-done.2 = bf16[32,16,768]{2,1,0:T(8,128)(2,1)S(1)} async-done(((bf16[32,16,768]{2,1,0:T(8,128)(2,1)}), bf16[32,16,768]{2,1,0:T(8,128)(2,1)S(1)}, u32[]{:S(2)}, u32[]{:S(2)}) %all-to-all-start.2) | async-done | bytes 786464 | tf_op jit(solution)/shard_map/while/body/all_to_all | solution.py:1507
  152.5 4.8 fusion.49
  159.1 13.6 %all-to-all-start.5 = ((bf16[32,48,768]{2,1,0:T(8,128)(2,1)}), bf16[32,48,768]{2,1,0:T(8,128)(2,1)}, u32[]{:S(2)}, u32[]{:S(2)}) async-start(bf16[32,48,768]{2,1,0:T(8,128)(2,1)} %bitcast.64), calls=%async_computation.5 | async-start | bytes 4718592 | tf_op jit(solution)/shard_map/all_to_all | solution.py:1507
  177.6 49.6 %all-to-all-done.5 = bf16[32,48,768]{2,1,0:T(8,128)(2,1)} async-done(((bf16[32,48,768]{2,1,0:T(8,128)(2,1)}), bf16[32,48,768]{2,1,0:T(8,128)(2,1)}, u32[]{:S(2)}, u32[]{:S(2)}) %all-to-all-start.5) | async-done | bytes 2359328 | tf_op jit(solution)/shard_map/all_to_all | solution.py:1507
  227.2 79.7 %forward.1 = (f32[2048,768]{1,0:T(8,128)}, bf16[2048,768]{1,0:T(8,128)(2,1)}, bf16[2048,2304]{1,0:T(8,128)(2,1)}, bf16[2048,768]{1,0:T(8,128)(2,1)}, f32[24,2,51...) custom-call(s32[2048,1]{1,0:T(8,128)} %copy.37.key_ref, bf16[1536,768]{1,0:T(8,128)(2,1)} %bitcast.8.found_ref, ...), custom_call_target="tpu_custom_call" | custom-call | flops 40000000000 | bytes 60000000 | tf_op jit(solution)/shard_map/forward/pallas_call | solution.py:1247
  306.8 78.0 %middle.1 = (bf16[2048,768]{1,0:T(8,128)(2,1)}, bf16[2048,768]{1,0:T(8,128)(2,1)}, bf16[2048,3072]{1,0:T(8,128)(2,1)}, bf16[2048,768]{1,0:T(8,128)(2,1)}, bf16[2...) custom-call(bf16[2048,768]{1,0:T(8,128)(2,1)} %get-tuple-element.311, ...), custom_call_target="tpu_custom_call" | custom-call | tf_op jit(solution)/shard_map/middle/pallas_call | solution.py:177
  386.7 32.1 %rest_gradients.1 = bf16[6912,768]{1,0:T(8,128)(2,1)} custom-call(bf16[2048,768]{1,0:T(8,128)(2,1)} %get-tuple-element.320.first_ref, bf16[2048,768]{1,0:T(8,128)(2,1)} %get-tuple-element.311.att_ref, bf16[2048,3072]{1,0:T(8,128)(2,1)} %get-tuple-element.321.up_ref, bf16[2048,768]{1,0:T(8,128)(2,1)} %get-tuple-element.322.normed_ref, ...), custom_call_target="tpu_custom_call" | custom-call | flops 22000001024 | bytes 50000000 | tf_op jit(solution)/shard_map/rest_gradients/pallas_call | solution.py:244
  418.8 82.4 %backward.1 = (bf16[2048,768]{1,0:T(8,128)(2,1)S(1)}, bf16[512,768]{1,0:T(8,128)(2,1)}, bf16[2304,768]{1,0:T(8,128)(2,1)}, f32[8,768]{1,0:T(8,128)}, f32[288,768]{1,0:T(8,128)}) custom-call(bf16[2048,2304]{1,0:T(8,128)(2,1)} %get-tuple-element.315.q_ref.k_ref.v_ref, bf16[2048,2304]{1,0:T(8,128)(2,1)} %get-tuple-element.315.q_ref.k_ref.v_ref, ...), custom_call_target="tpu_custom_call" | custom-call | flops 60000002048 | bytes 60000000 | tf_op jit(solution)/shard_map/backward/pallas_call | solution.py:1383
  503.0 10.0 %all-to-all-start.7 = ((f32[32,1,288]{2,1,0:T(1,128)}), f32[32,1,288]{2,1,0:T(1,128)}, u32[]{:S(2)}, u32[]{:S(2)}) async-start(f32[32,1,288]{2,1,0:T(1,128)} %all_to_all.49), calls=%async_computation.7 | async-start | bytes 98304 | tf_op jit(solution)/shard_map/all_to_all | solution.py:1507
  513.0 7.2 %fusion.7 = bf16[1536,768]{1,0:T(8,128)(2,1)} fusion(bf16[2048,768]{1,0:T(8,128)(2,1)S(1)} %get-tuple-element.582, s32[2048]{0:T(1024)S(1)} %copy-done.23), kind=kOutput, calls=%fused_computation.28 | convolution fusion | flops 4836163584 | bytes 5513216 | tf_op jit(solution)/shard_map/dot_general | solution.py:48
  520.3 6.0 all-to-all-start.6
  527.5 72.0 %homecoming.1 = (f32[472,768]{1,0:T(8,128)S(1)}, f32[288,768]{1,0:T(8,128)S(1)}) custom-call(bf16[4,2,2,2,16,768]{5,4,3,2,1,0:T(8,128)(2,1)S(1)} %bitcast.52, bf16[8,288,768]{2,1,0:T(8,128)(2,1)S(1)} %bitcast.51), custom_call_target="tpu_custom_call" | custom-call | bytes 200000000 | tf_op jit(solution)/shard_map/homecoming/pallas_call | solution.py:1103
  604.0 3.3 fusion.18
  607.3 34.0 %while.25 = (s32[]{:T(128)}, f32[472,768]{1,0:T(8,128)S(1)}, s32[]{:T(128)}, s32[2048]{0:T(1024)S(1)}, s32[2048]{0:T(1024)S(1)}, /*index=5*/s32[2048]{0:T(1024)S...) while((s32[]{:T(128)}, f32[472,768]{1,0:T(8,128)S(1)}, ...), condition=%wide.region_15.16_spmd, body=%wide.region_11.15_spmd.sunk | while | flops 1987018240 | bytes 12169475 | solution.py:1646
  608.1 4.9 convolution_convert_fusion.7
  613.0 6.7 %all-to-all-start.3 = ((bf16[32,16,768]{2,1,0:T(8,128)(2,1)}), bf16[32,16,768]{2,1,0:T(8,128)(2,1)S(1)}, u32[]{:S(2)}, u32[]{:S(2)}) async-start(bf16[32,16,768]{2,1,0:T(8,128)(2,1)} %bitcast.49), calls=%async_computation.3 | async-start | bytes 1572864 | tf_op jit(solution)/shard_map/while/body/all_to_all | solution.py:1507
  619.7 20.6 %all-to-all-done.3 = bf16[32,16,768]{2,1,0:T(8,128)(2,1)S(1)} async-done(((bf16[32,16,768]{2,1,0:T(8,128)(2,1)}), bf16[32,16,768]{2,1,0:T(8,128)(2,1)S(1)}, u32[]{:S(2)}, u32[]{:S(2)}) %all-to-all-start.3) | async-done | bytes 786464 | tf_op jit(solution)/shard_map/while/body/all_to_all | solution.py:1507
  641.3 5.4 fusion.17
  (131 shorter events, 36.9 us)
Async XLA Ops:
  11.4 161.3 %copy-start.22 = (s32[2048]{0:T(1024)}, s32[2048]{0:T(1024)S(1)}, u32[]{:S(2)}) copy-start(s32[2048]{0:T(1024)S(1)} %get-tuple-element.389) | copy-start | bytes 24580
  17.2 103.3 %all-to-all-start.4 = ((f32[32,1,353]{2,1,0:T(1,128)}), f32[32,1,353]{2,1,0:T(1,128)S(1)}, u32[]{:S(2)}, u32[]{:S(2)}) async-start(f32[32,1,353]{2,1,0:T(1,128)} %all_to_all.44), calls=%async_computation.4 | async-start | bytes 98304 | tf_op jit(solution)/shard_map/all_to_all | solution.py:1507
  129.3 23.2 %all-to-all-start.2 = ((bf16[32,16,768]{2,1,0:T(8,128)(2,1)}), bf16[32,16,768]{2,1,0:T(8,128)(2,1)S(1)}, u32[]{:S(2)}, u32[]{:S(2)}) async-start(bf16[32,16,768]{2,1,0:T(8,128)(2,1)} %bitcast.45), calls=%async_computation.2 | async-start | bytes 1572864 | tf_op jit(solution)/shard_map/while/body/all_to_all | solution.py:1507
  159.1 16.3 %copy-start.5 = (s32[2048]{0:T(1024)}, s32[2048]{0:T(1024)S(1)}, u32[]{:S(2)}) copy-start(s32[2048]{0:T(1024)S(1)} %get-tuple-element.596) | copy-start | bytes 24580
  159.1 14.9 %copy-start.21 = (s32[2048]{0:T(1024)S(1)}, s32[2048]{0:T(1024)}, u32[]{:S(2)}) copy-start(s32[2048]{0:T(1024)} %param.23) | copy-start | bytes 24580
  159.1 68.1 %copy-start.10 = (bf16[2048,768]{1,0:T(8,128)(2,1)S(1)}, bf16[2048,768]{1,0:T(8,128)(2,1)}, u32[]{:S(2)}) copy-start(bf16[2048,768]{1,0:T(8,128)(2,1)} %get-tuple-element.308.extra_ref) | copy-start | bytes 9437188
  159.1 68.1 %all-to-all-start.5 = ((bf16[32,48,768]{2,1,0:T(8,128)(2,1)}), bf16[32,48,768]{2,1,0:T(8,128)(2,1)}, u32[]{:S(2)}, u32[]{:S(2)}) async-start(bf16[32,48,768]{2,1,0:T(8,128)(2,1)} %bitcast.64), calls=%async_computation.5 | async-start | bytes 4718592 | tf_op jit(solution)/shard_map/all_to_all | solution.py:1507
  418.8 83.3 %copy-start.20 = (f32[9216]{0:T(1024)S(1)}, f32[9216]{0:T(1024)}, u32[]{:S(2)}) copy-start(f32[9216]{0:T(1024)} %custom-call) | copy-start | bytes 110596
  418.8 94.2 %copy-start.23 = (s32[2048]{0:T(1024)S(1)}, s32[2048]{0:T(1024)}, u32[]{:S(2)}) copy-start(s32[2048]{0:T(1024)} %copy-done.22) | copy-start | bytes 24580
  501.3 11.7 %copy-start.8 = (bf16[2048,768]{1,0:T(8,128)(2,1)}, bf16[2048,768]{1,0:T(8,128)(2,1)S(1)}, u32[]{:S(2)}) copy-start(bf16[2048,768]{1,0:T(8,128)(2,1)S(1)} %get-tuple-element.582) | copy-start | bytes 9437188
  503.0 17.3 %all-to-all-start.7 = ((f32[32,1,288]{2,1,0:T(1,128)}), f32[32,1,288]{2,1,0:T(1,128)}, u32[]{:S(2)}, u32[]{:S(2)}) async-start(f32[32,1,288]{2,1,0:T(1,128)} %all_to_all.49), calls=%async_computation.7 | async-start | bytes 98304 | tf_op jit(solution)/shard_map/all_to_all | solution.py:1507
  520.2 6.1 copy-start
  520.3 83.6 %all-to-all-start.6 = ((bf16[32,48,768]{2,1,0:T(8,128)(2,1)}), bf16[32,48,768]{2,1,0:T(8,128)(2,1)}, u32[]{:S(2)}, u32[]{:S(2)}) async-start(bf16[32,48,768]{2,1,0:T(8,128)(2,1)} %bitcast.65), calls=%async_computation.6 | async-start | bytes 4718592 | tf_op jit(solution)/shard_map/all_to_all | solution.py:1507
  527.4 73.1 %copy-start.7 = (f32[768,288]{0,1:T(8,128)S(1)}, f32[768,288]{0,1:T(8,128)}, u32[]{:S(2)}) copy-start(f32[768,288]{0,1:T(8,128)} %param.30) | copy-start | bytes 2654212
  527.4 73.1 %copy-start.15 = (f32[768,288]{0,1:T(8,128)S(1)}, f32[768,288]{0,1:T(8,128)}, u32[]{:S(2)}) copy-start(f32[768,288]{0,1:T(8,128)} %param.32) | copy-start | bytes 2654212
  527.4 73.1 %copy-start.16 = (f32[768,288]{0,1:T(8,128)S(1)}, f32[768,288]{0,1:T(8,128)}, u32[]{:S(2)}) copy-start(f32[768,288]{0,1:T(8,128)} %param.31) | copy-start | bytes 2654212
  527.5 73.1 %copy-start.17 = (f32[288,768]{1,0:T(8,128)S(1)}, f32[288,768]{1,0:T(8,128)}, u32[]{:S(2)}) copy-start(f32[288,768]{1,0:T(8,128)} %get-tuple-element.334) | copy-start | bytes 2654212
  603.3 4.0 copy-start.26
  603.9 3.4 copy-start.6
  603.9 3.4 copy-start.12
  603.9 3.4 copy-start.14
  613.0 27.3 %all-to-all-start.3 = ((bf16[32,16,768]{2,1,0:T(8,128)(2,1)}), bf16[32,16,768]{2,1,0:T(8,128)(2,1)S(1)}, u32[]{:S(2)}, u32[]{:S(2)}) async-start(bf16[32,16,768]{2,1,0:T(8,128)(2,1)} %bitcast.49), calls=%async_computation.3 | async-start | bytes 1572864 | tf_op jit(solution)/shard_map/while/body/all_to_all | solution.py:1507
  641.3 5.4 copy-start.4
  641.3 5.4 copy-start.9
  (12 other events, 25.0 us)
